TPU v7x, 128 devices: a whole 4x4x4 slice. The times are simulated.
128 devices in a mesh: grp: 4 (over z_lo, core), blk: 32 (over y, x, z_hi).
Axes of the slice: x: 4, y: 4, z: 4 (z_hi: 2, z_lo: 2; z = z_hi * 2 + z_lo), core: 2. Of those that a mesh axis runs over, the one named last changes fastest.
Arguments:
- embeddings: float32 [4, 4, 32, 128, 768], P(None, 'grp', 'blk')
- cluster_ids: int32 [4, 16384], P('grp'), may hold values from 0 to 63, as said below
Outputs:
- best_match: float32 [4, 16384], P('grp', 'blk')
Inputs may be any that keep to these rules, and one draw needn't show every extreme that they name: `cluster_ids`: along each group's row the ids never fall; group g holds clusters g * 16 to (g + 1) * 16 - 1, each with one point or more, and the largest of them has exactly 9216 points.
All inputs are finite; a program needn't handle non-finite values.
Results may differ from a plain program's by a relative error of at most 0.0003.
Values may be sent and summed in bfloat16 or wider, within the bound.
A program may use at most 128 MiB of HBM per device.

v0:
```python
import functools

import jax
import jax.numpy as jnp
from jax import lax
from jax.experimental import pallas as pl
from jax.experimental.pallas import tpu as pltpu
from jax.sharding import PartitionSpec as P

MESH = pl.DeviceIdType.MESH
D = 768
SLOTS = 5
PIECE = 64
STEPS = 8

SRC = [[0, 3, 0, 0], [3, 0, 0, 0], [0, 0, 4, 0], [0, 0, 4, 0], [0, 4, 1, 0], [4, 0, 2, 0], [0, 3, 0, 0], [3, 0, 0, 0],
       [3, 0, 0, 3], [0, 3, 0, 3], [2, 4, 0, 0], [4, 1, 0, 0], [2, 0, 4, 0], [0, 1, 4, 0], [4, 0, 0, 3], [0, 4, 0, 3]]
DEP = [[1, 1, 1, 2], [1, 1, 1, 2], [1, 2, 1, 1], [2, 1, 1, 1], [1, 2, 2, 1], [2, 1, 2, 1], [1, 2, 1, 2], [2, 1, 1, 2],
       [2, 2, 1, 2], [2, 2, 1, 2], [2, 1, 2, 1], [1, 2, 2, 1], [2, 1, 1, 1], [1, 2, 1, 1], [2, 1, 1, 1], [1, 2, 1, 1]]
BLK = [[1, 3, 4, 8], [2, 0, 5, 9], [3, 5, 6, 14], [4, 2, 7, 15], [5, 11, 12, 0], [10, 4, 13, 1], [7, 1, 10, 14],
       [0, 6, 11, 15], [13, 7, 12, 5], [6, 12, 13, 4], [8, 9, 2, 6], [8, 9, 3, 7], [14, 15, 0, 8], [14, 15, 1, 9],
       [11, 13, 2, 10], [12, 10, 3, 11]]
IDX = [[1, 1, 1, 1], [1, 1, 1, 1], [2, 2, 1, 1], [2, 2, 1, 1], [3, 1, 1, 2], [1, 3, 1, 2], [2, 3, 2, 2], [3, 2, 2, 2],
       [2, 3, 2, 4], [3, 3, 3, 4], [2, 2, 3, 4], [3, 3, 3, 4], [3, 3, 4, 4], [4, 4, 4, 4], [3, 4, 4, 3], [4, 4, 4, 4]]
HOLD = [[0, 1, 4, 7, 12], [1, 0, 5, 6, 13], [2, 1, 3, 10, 14], [3, 0, 2, 11, 15], [4, 0, 3, 5, 9], [5, 1, 2, 4, 8],
        [6, 2, 7, 9, 10], [7, 3, 6, 8, 11], [8, 0, 10, 11, 12], [9, 1, 10, 11, 13], [10, 5, 6, 14, 15], [11, 4, 7, 14, 15],
        [12, 4, 8, 9, 15], [13, 5, 8, 9, 14], [14, 2, 6, 12, 13], [15, 3, 7, 12, 13]]
PAIRS = [[[(1, 3), (1, 4), (3, 4)], [(0, 1), (0, 2), (1, 2)]], [[(2, 1), (2, 4), (1, 4)], [(0, 1), (0, 3), (3, 4)]],
         [[(1, 3), (3, 4), (2, 3), (2, 4)], [(0, 1), (0, 2), (1, 2)]],
         [[(2, 3), (2, 1), (1, 3)], [(0, 3), (3, 4), (0, 1)]], [[(4, 0), (4, 1), (0, 2), (1, 2)], [(0, 3), (1, 3)]],
         [[(2, 0), (4, 1), (2, 1)], [(0, 1), (0, 3), (1, 3)]], [[(1, 3), (1, 4), (3, 4)], [(0, 3), (2, 0), (2, 1)]],
         [[(2, 3), (2, 4), (3, 4)], [(2, 0), (1, 2), (1, 0)]],
         [[(2, 3), (2, 1), (0, 1), (3, 1)], [(4, 2), (4, 0), (2, 0)]],
         [[(4, 1), (4, 0), (4, 3), (1, 3)], [(1, 0), (1, 2), (0, 2)]],
         [[(3, 4), (3, 1), (4, 1)], [(2, 0), (1, 2), (1, 0)]], [[(1, 0), (3, 1), (3, 2)], [(4, 0), (4, 2), (2, 0)]],
         [[(3, 4), (4, 1), (0, 1)], [(4, 0), (4, 2), (0, 2)]], [[(3, 4), (4, 1), (1, 2)], [(4, 0), (4, 2), (0, 2)]],
         [[(3, 4), (3, 1), (4, 1)], [(2, 0), (1, 2), (1, 0)]], [[(3, 4), (3, 1), (4, 1)], [(3, 2), (2, 1), (2, 0)]]]
NEED = [[[1, 3, 4], [0, 1, 2]], [[1, 2, 4], [0, 1, 3, 4]], [[1, 2, 3, 4], [0, 1, 2]], [[1, 2, 3], [0, 1, 3, 4]],
        [[0, 1, 2, 4], [0, 1, 3]], [[0, 1, 2, 4], [0, 1, 3]], [[1, 3, 4], [0, 1, 2, 3]], [[2, 3, 4], [0, 1, 2]],
        [[0, 1, 2, 3], [0, 2, 4]], [[0, 1, 3, 4], [0, 1, 2]], [[1, 3, 4], [0, 1, 2]], [[0, 1, 2, 3], [0, 2, 4]],
        [[0, 1, 3, 4], [0, 2, 4]], [[1, 2, 3, 4], [0, 2, 4]], [[1, 3, 4], [0, 1, 2]], [[1, 3, 4], [0, 1, 2, 3]]]

REL = (0, 3, 1, 2)


def word(digits, base):
    total = 0
    for digit in reversed(digits):
        total = total * base + digit
    return total


def look_up(index, words):
    got = jnp.int32(words[0])
    for k in range(1, len(words)):
        got = jnp.where(index == k, jnp.int32(words[k]), got)
    return got


def digits_of(value, base, count):
    out = []
    for _ in range(count):
        out.append(value % base)
        value = value // base
    return out


def kernel(emb, ids_in, out, x, units, stage, ids_got, ids_rows, ids_cols, row_best, col_best, row_line, part, parts_got,
           relay,
           load_sem, id_send, id_recv, z_send, z_recv, relay_send, relay_recv, f_send, f_recv, c_send, c_recv, r_send, r_recv):
    grp, blk = lax.axis_index("grp"), lax.axis_index("blk")
    h, zl = grp % 2, grp // 2
    p, zh = blk // 2, blk % 2
    z = zh * 2 + zl
    px, py = p % 4, p // 4

    def device(z_of, core, chip):
        return ((z_of % 2) * 2 + core, chip * 2 + z_of // 2)

    def group_of(z_of):
        return (z_of % 2) * 2 + z_of // 2

    near = [py * 4 + (px + 1) % 4, py * 4 + (px + 3) % 4, ((py + 1) % 4) * 4 + px, ((py + 3) % 4) * 4 + px]
    first = look_up(p, [word(SRC[c], 8) + 4096 * word(DEP[c], 4) for c in range(16)])
    src = digits_of(first, 8, 4)
    dep = digits_of(first // 4096, 4, 4)
    held = [p] + digits_of(look_up(p, [word(BLK[c], 16) for c in range(16)]), 16, 4)
    third = look_up(p, [word(IDX[c], 8) + 4096 * word(HOLD[c][1:], 16) for c in range(16)])
    place = [jnp.int32(0)] + digits_of(third, 8, 4)
    holders = [p] + digits_of(third // 4096, 16, 4)
    lists = []
    for c in range(16):
        for core in range(2):
            flat = [slot for pair in PAIRS[c][core] for slot in pair]
            lists.append(len(PAIRS[c][core]) + 8 * word(flat + [0] * (8 - len(flat)), 8))
    todo = look_up(p * 2 + h, lists)
    pair_count = todo % 8
    todo = digits_of(todo // 8, 8, 8)

    needs = [[sum(1 << slot for slot in NEED[c][core]) for core in range(2)] for c in range(16)]
    need = digits_of(look_up(p * 2 + h, [needs[c][core] for c in range(16) for core in range(2)]), 2, SLOTS)
    sibling_need = digits_of(look_up(p * 2 + h, [needs[c][1 - core] for c in range(16) for core in range(2)]), 2, SLOTS)

    sibling = device(z, 1 - h, p)
    owner_grp = zl * 2 + zh
    mine = h == zh

    loads = []
    for k, rel in enumerate((0, 1, 3, 2)):
        loads.append(pltpu.make_async_copy(emb.at[group_of((z + rel) % 4)], stage.at[k], load_sem.at[k]))
        loads[-1].start()

    barrier = pltpu.get_barrier_semaphore()
    for rel in (1, 3):
        pl.semaphore_signal(barrier, inc=1, device_id=device((z + rel) % 4, h, p), device_id_type=MESH)
    for d in range(4):
        pl.semaphore_signal(barrier, inc=1, device_id=device(z, h, near[d]), device_id_type=MESH)
    pl.semaphore_signal(barrier, inc=1, device_id=sibling, device_id_type=MESH)
    from_z = 2 * h + zl
    for k in range(SLOTS):
        for core in range(2):
            def tell():
                pl.semaphore_signal(barrier, inc=1, device_id=device(from_z, core, holders[k]), device_id_type=MESH)
            if k == 0:
                pl.when(jnp.logical_not(jnp.logical_and(mine, h == core)))(tell)
            else:
                tell()

    def normalise(k):
        loads[k].wait()
        v = stage[k]
        total = jnp.sum(v * v, axis=-1, keepdims=True)
        return (v / jnp.sqrt(total + 1e-06)).astype(jnp.bfloat16)

    own_rows = pl.multiple_of(h * 128, 128)
    x[0, pl.ds(own_rows, 128), :] = normalise(0)
    pl.semaphore_wait(barrier, jnp.where(mine, 16, 17))

    def remote(src_ref, dst_ref, send_sem, recv_sem, to):
        return pltpu.make_async_remote_copy(
            src_ref=src_ref, dst_ref=dst_ref, send_sem=send_sem, recv_sem=recv_sem, device_id=to, device_id_type=MESH)

    def part_rows(t):
        return pl.ds(pl.multiple_of((t // 2) * 256 + h * 128 + (t % 2) * PIECE, PIECE), PIECE)

    def forward(d, t):
        rows = part_rows(t)
        return remote(x.at[src[d], rows, :], x.at[1 + (d ^ 1), rows, :], f_send.at[d, t], f_recv.at[d ^ 1, t],
                      device(z, h, near[d]))

    def arrival(s, t):
        rows = part_rows(t)
        return remote(x.at[s, rows, :], x.at[s, rows, :], f_send.at[s - 1, t], f_recv.at[s - 1, t],
                      device(z, h, near[s - 1]))

    def swap(k, half):
        rows = pl.ds(pl.multiple_of(k * 256 + h * 128 + half * 64, 64), 64)
        return remote(units.at[k - 1, pl.ds(half * 64, 64), :], x.at[0, rows, :], z_send.at[k - 1, half],
                      z_recv.at[k - 1, half], device((z + (1, 3, 2)[k - 1]) % 4, h, p))

    between = device((z + jnp.where(h == 0, 1, 3)) % 4, h, p)

    def relay_in(half):
        rows = pl.ds(half * 64, 64)
        return remote(units.at[2, rows, :], relay.at[rows, :], relay_send.at[0, half], relay_recv.at[half], between)

    def relay_out(half):
        rows = pl.ds(pl.multiple_of(3 * 256 + h * 128 + half * 64, 64), 64)
        return remote(relay.at[pl.ds(half * 64, 64), :], x.at[0, rows, :], relay_send.at[1, half], z_recv.at[2, half],
                      between)

    def share_rows(t, core):
        return pl.ds(pl.multiple_of((t // 2) * 256 + core * 128 + (t % 2) * 64, 64), 64)

    def share(s, t):
        rows = share_rows(t, h)
        return remote(x.at[s, rows, :], x.at[s, rows, :], c_send.at[s, t], c_recv.at[s, t], sibling)

    def shared(s, t):
        rows = share_rows(t, 1 - h)
        return remote(x.at[s, rows, :], x.at[s, rows, :], c_send.at[s, t], c_recv.at[s, t], sibling)

    def give(s, t):
        pl.when(sibling_need[s] == 1)(lambda: share(s, t).start())

    def send_own(t):
        for d in range(4):
            pl.when(src[d] == 0)(lambda d=d: forward(d, t).start())

    def send_held(t):
        for d in range(4):
            pl.when(src[d] != 0)(lambda d=d: forward(d, t).start())

    def receive(links, t):
        for s in range(1, SLOTS):
            pl.when(dep[s - 1] == links)(lambda s=s: arrival(s, t).wait_recv())

    def give_held(links, t):
        for s in range(1, SLOTS):
            pl.when(dep[s - 1] == links)(lambda s=s: give(s, t))

    for t in range(2):
        send_own(t)
    units[0] = normalise(1)
    for half in range(2):
        swap(1, half).start()
    units[1] = normalise(2)
    for half in range(2):
        swap(2, half).start()
    units[2] = normalise(3)
    for half in range(2):
        relay_in(half).start()
    ids_copy = remote(ids_in, ids_got, id_send, id_recv, sibling)
    ids_copy.start()
    give(0, 0)
    give(0, 1)
    row_best[...] = jnp.full_like(row_best, -1.0)
    col_best[...] = jnp.full_like(col_best, -1.0)
    row_line[...] = jnp.full_like(row_line, -1.0)

    ids_copy.wait_recv()
    ids_cols[...] = jnp.zeros_like(ids_cols)
    for s in range(SLOTS):
        for t in range(4):
            for core in range(2):
                unit = held[s] * 8 + 2 * ((z + REL[t]) % 4) + core
                got = jnp.where(mine, ids_in[pl.ds(unit, 1), :], ids_got[pl.ds(unit, 1), :])
                ids_cols[pl.ds(s * 8 + 2 * t + core, 1), :] = got.astype(jnp.float32)
    turned = ids_cols[...].T
    for j in range(SLOTS * 8):
        ids_rows[j] = jnp.broadcast_to(turned[:, j:j + 1], (128, 128))

    def strip(a, t, b, count, diagonal=False):
        sim = lax.dot_general(x[b, 0:256 * count, :], x[a, 256 * t:256 * t + 256, :], (((1,), (1,)), ((), ())),
                              preferred_element_type=jnp.float32)
        col_ids = [ids_cols[pl.ds(a * 8 + 2 * t + c, 1), :] for c in range(2)]
        downs = [col_best[a * 8 + 2 * t + c] for c in range(2)]
        for r in range(4 * count):
            unit, first_row = b * 8 + r // 2, 64 * (r % 2)
            row_ids = ids_rows[unit, first_row:first_row + 64]
            best = row_best[unit, first_row:first_row + 64]
            for c in range(2):
                keep = row_ids == col_ids[c]
                if diagonal and r // 4 == t:
                    row = lax.broadcasted_iota(jnp.int32, (64, 128), 0) + 64 * (r % 4)
                    col = lax.broadcasted_iota(jnp.int32, (64, 128), 1) + 128 * c
                    keep = jnp.logical_and(keep, row != col)
                kept = jnp.where(keep, sim[64 * r:64 * r + 64, 128 * c:128 * c + 128], jnp.float32(-1.0))
                downs[c] = jnp.maximum(downs[c], jnp.max(kept.reshape(8, 8, 128), axis=0))
                best = jnp.maximum(best, kept)
            row_best[unit, first_row:first_row + 64] = best
        for c in range(2):
            col_best[a * 8 + 2 * t + c] = downs[c]

    def compare(t, j):
        a, b = todo[0], todo[1]
        for k in range(1, 4):
            a = jnp.where(j == k, todo[2 * k], a)
            b = jnp.where(j == k, todo[2 * k + 1], b)
        strip(a, t, b, t + 1)
        if t:
            strip(b, t, a, t)

    def own_pair(t):
        pl.when(h == 1)(lambda: strip(0, t, 0, t + 1, diagonal=True))

    def wait_shared(m):
        for s in range(SLOTS):
            @pl.when(need[s] == 1)
            def _():
                for half in range(2):
                    shared(s, 2 * m + half).wait_recv()

    def own_piece_ready(t):
        send_own(t)
        give(0, t)

    def pass_on(k):
        receive(1, k - 1)
        send_held(k - 1)
        give_held(1, k - 1)

    def take(t):
        receive(2, t)
        give_held(2, t)

    pass_on(1)
    swap(1, 0).wait_recv()
    own_piece_ready(2)
    pass_on(2)
    swap(1, 1).wait_recv()
    own_piece_ready(3)
    swap(2, 0).wait_recv()
    own_piece_ready(4)
    pass_on(3)
    for half in range(2):
        relay_in(half).wait_recv()
        relay_out(half).start()
    swap(2, 1).wait_recv()
    own_piece_ready(5)
    take(0)
    pass_on(4)
    take(1)
    for m in range(2):
        @pl.loop(5 + 2 * m, 7 + 2 * m)
        def _(k):
            pass_on(k)

            @pl.when(k == 5)
            def _():
                for half in range(2):
                    relay_out(half).wait_recv()
                    own_piece_ready(6 + half)
            first = 2 * (k - 5 - 2 * m)
            pl.when(first == 0)(lambda: wait_shared(m))

            @pl.loop(first, jnp.minimum(first + 2, pair_count))
            def _(j):
                compare(m, j)
            take(k - 3)
        own_pair(m)
    for m in (2, 3):
        wait_shared(m)

        @pl.loop(0, pair_count)
        def _(j):
            compare(m, j)
        own_pair(m)
        if m == 2:
            take(6)
            take(7)

    for s in range(SLOTS):
        @pl.when(need[s] == 1)
        def _():
            for unit in range(s * 8, s * 8 + 8):
                row_line[unit:unit + 1, :] = jnp.max(row_best[unit].T, axis=0, keepdims=True)

    for s in range(SLOTS):
        for t in range(4):
            z_of = (z + REL[t]) % 4
            for core in range(2):
                j = s * 8 + 2 * t + core
                both = jnp.maximum(row_line[j:j + 1, :], jnp.max(col_best[j], axis=0, keepdims=True))
                part[s * 2 + z_of // 2, pl.ds(2 * (z_of % 2) + core, 1), :] = both
        for half in range(2):
            copy = remote(part.at[s * 2 + half], parts_got.at[place[s] * 2 + h], r_send.at[s * 2 + half],
                          r_recv.at[place[s] * 2 + h], (owner_grp, held[s] * 2 + half))
            if s == 0:
                keep_it = jnp.logical_and(mine, zh == half)
                pl.when(jnp.logical_not(keep_it))(copy.start)

                @pl.when(keep_it)
                def _():
                    parts_got[h] = part[half]
            else:
                copy.start()

    best = None
    for k in range(2 * SLOTS):
        got = remote(parts_got.at[k], parts_got.at[k], r_send.at[k], r_recv.at[k], sibling)
        if k < 2:
            pl.when(jnp.logical_not(jnp.logical_and(mine, h == k)))(got.wait_recv)
        else:
            got.wait_recv()
        best = parts_got[k] if best is None else jnp.maximum(best, parts_got[k])
    out[...] = best

    ids_copy.wait_send()
    for half in range(2):
        for copy in (swap(1, half), swap(2, half), relay_in(half), relay_out(half)):
            copy.wait_send()
    for d in range(4):
        for t in range(STEPS):
            forward(d, t).wait_send()
    for s in range(SLOTS):
        for t in range(8):
            pl.when(sibling_need[s] == 1)(lambda s=s, t=t: share(s, t).wait_send())
        for half in range(2):
            copy = remote(part.at[s * 2 + half], parts_got.at[place[s] * 2 + h], r_send.at[s * 2 + half],
                          r_recv.at[place[s] * 2 + h], (owner_grp, held[s] * 2 + half))
            if s == 0:
                pl.when(jnp.logical_not(jnp.logical_and(mine, zh == half)))(copy.wait_send)
            else:
                copy.wait_send()


def on_device(embeddings, cluster_ids):
    emb = embeddings.reshape(4, 128, D)
    ids = cluster_ids.reshape(128, 128)
    dma = pltpu.SemaphoreType.DMA
    best = pl.pallas_call(
        kernel,
        out_shape=jax.ShapeDtypeStruct((4, 128), jnp.float32),
        in_specs=[pl.BlockSpec(memory_space=pl.ANY), pl.BlockSpec(memory_space=pltpu.VMEM)],
        out_specs=pl.BlockSpec(memory_space=pltpu.VMEM),
        scratch_shapes=[
            pltpu.VMEM((SLOTS, 1024, D), jnp.bfloat16),
            pltpu.VMEM((3, 128, D), jnp.bfloat16),
            pltpu.VMEM((4, 128, D), jnp.float32),
            pltpu.VMEM((128, 128), jnp.int32),
            pltpu.VMEM((SLOTS * 8, 128, 128), jnp.float32),
            pltpu.VMEM((128, 128), jnp.float32),
            pltpu.VMEM((SLOTS * 8, 128, 128), jnp.float32),
            pltpu.VMEM((SLOTS * 8, 8, 128), jnp.float32),
            pltpu.VMEM((SLOTS * 8, 128), jnp.float32),
            pltpu.VMEM((2 * SLOTS, 4, 128), jnp.float32),
            pltpu.VMEM((2 * SLOTS, 4, 128), jnp.float32),
            pltpu.VMEM((128, D), jnp.bfloat16),
            dma((4,)), dma, dma, dma((3, 2)), dma((3, 2)), dma((2, 2)), dma((2,)), dma((4, STEPS)), dma((4, STEPS)),
            dma((SLOTS, 8)), dma((SLOTS, 8)), dma((2 * SLOTS,)), dma((2 * SLOTS,)),
        ],
        compiler_params=pltpu.CompilerParams(
            collective_id=0, has_side_effects=True, vmem_limit_bytes=60 * 1024 * 1024),
        cost_estimate=pl.CostEstimate(flops=7 * 10**9, bytes_accessed=2 * 10**6, transcendentals=0),
        name="best_match",
    )(emb, ids)
    return best.reshape(1, 512)


def solution(mesh):
    placed = (P(None, "grp", "blk", None, None), P("grp", None))
    return jax.shard_map(
        on_device, mesh=mesh, in_specs=placed, out_specs=P("grp", "blk"), check_vma=False
    )
```

profile of v0, /device:TPU:1, one launch (start us, length us, event | category | flops | bytes accessed | tf_op | source)
XLA Modules:
  0.0 46.9 jit_solution(3622746888234266965)
XLA Ops:
  0.0 45.6 %best_match.1 = f32[4,128]{1,0:T(4,128)} custom-call(f32[4,128,768]{2,1,0:T(8,128)} %bitcast.4, s32[128,128]{1,0:T(8,128)} %bitcast.5), custom_call_target="tpu_custom_call" | custom-call | flops 7000000000 | bytes 2000000 | tf_op jit(solution)/shard_map/best_match/pallas_call | solution.py:392
  45.6 1.3 %copy.4 = f32[1,512]{1,0:T(1,128)} copy(f32[1,512]{1,0:T(1,128)} %bitcast.3) | data formatting | bytes 4096
where the time goes:
time: 47.1 us; the launch traced here: 46.9 us
  Pallas kernels  45.6 us (97%)
  local copies, waits for them, and re-layouts  1.26 us (3%)
    pallas_call x1, Pallas kernels, on_device(): pl.pallas_call(kernel, out_shape=jax.ShapeDtypeStruct((4, 128), jnp.float...  45.6 us
    unnamed x1, local copies, waits for them, and re-layouts  1.26 us

commit v1 on v0

--- a/solution.py
+++ b/solution.py
@@ -65,9 +65,9 @@
     return out
 
 
-def kernel(emb, ids_in, out, x, units, stage, ids_got, ids_rows, ids_cols, row_best, col_best, row_line, part, parts_got,
+def kernel(emb, ids_in, out, x, units, stage, ids_own, ids_got, ids_rows, ids_cols, row_best, col_best, row_line, part, parts_got,
            relay,
-           load_sem, id_send, id_recv, z_send, z_recv, relay_send, relay_recv, f_send, f_recv, c_send, c_recv, r_send, r_recv):
+           load_sem, ids_sem, id_send, id_recv, z_send, z_recv, relay_send, relay_recv, f_send, f_recv, c_send, c_recv, r_send, r_recv):
     grp, blk = lax.axis_index("grp"), lax.axis_index("blk")
     h, zl = grp % 2, grp // 2
     p, zh = blk // 2, blk % 2
@@ -109,6 +109,9 @@
     for k, rel in enumerate((0, 1, 3, 2)):
         loads.append(pltpu.make_async_copy(emb.at[group_of((z + rel) % 4)], stage.at[k], load_sem.at[k]))
         loads[-1].start()
+
+    ids_load = pltpu.make_async_copy(ids_in, ids_own, ids_sem)
+    ids_load.start()
 
     barrier = pltpu.get_barrier_semaphore()
     for rel in (1, 3):
@@ -218,39 +221,37 @@
     col_best[...] = jnp.full_like(col_best, -1.0)
     row_line[...] = jnp.full_like(row_line, -1.0)
 
+    ids_load.wait()
     ids_copy.wait_recv()
     ids_cols[...] = jnp.zeros_like(ids_cols)
     for s in range(SLOTS):
         for t in range(4):
             for core in range(2):
                 unit = held[s] * 8 + 2 * ((z + REL[t]) % 4) + core
-                got = jnp.where(mine, ids_in[pl.ds(unit, 1), :], ids_got[pl.ds(unit, 1), :])
+                got = jnp.where(mine, ids_own[pl.ds(unit, 1), :], ids_got[pl.ds(unit, 1), :])
                 ids_cols[pl.ds(s * 8 + 2 * t + core, 1), :] = got.astype(jnp.float32)
     turned = ids_cols[...].T
     for j in range(SLOTS * 8):
         ids_rows[j] = jnp.broadcast_to(turned[:, j:j + 1], (128, 128))
 
     def strip(a, t, b, count, diagonal=False):
-        sim = lax.dot_general(x[b, 0:256 * count, :], x[a, 256 * t:256 * t + 256, :], (((1,), (1,)), ((), ())),
+        sim = lax.dot_general(x[a, 256 * t:256 * t + 256, :], x[b, 0:256 * count, :], (((1,), (1,)), ((), ())),
                               preferred_element_type=jnp.float32)
-        col_ids = [ids_cols[pl.ds(a * 8 + 2 * t + c, 1), :] for c in range(2)]
-        downs = [col_best[a * 8 + 2 * t + c] for c in range(2)]
-        for r in range(4 * count):
-            unit, first_row = b * 8 + r // 2, 64 * (r % 2)
+        for r in range(4):
+            unit, first_row = a * 8 + 2 * t + r // 2, 64 * (r % 2)
             row_ids = ids_rows[unit, first_row:first_row + 64]
             best = row_best[unit, first_row:first_row + 64]
-            for c in range(2):
-                keep = row_ids == col_ids[c]
-                if diagonal and r // 4 == t:
-                    row = lax.broadcasted_iota(jnp.int32, (64, 128), 0) + 64 * (r % 4)
-                    col = lax.broadcasted_iota(jnp.int32, (64, 128), 1) + 128 * c
+            for c in range(2 * count):
+                keep = row_ids == ids_cols[pl.ds(b * 8 + c, 1), :]
+                if diagonal and c // 2 == t:
+                    row = lax.broadcasted_iota(jnp.int32, (64, 128), 0) + 64 * r
+                    col = lax.broadcasted_iota(jnp.int32, (64, 128), 1) + 128 * (c % 2)
                     keep = jnp.logical_and(keep, row != col)
                 kept = jnp.where(keep, sim[64 * r:64 * r + 64, 128 * c:128 * c + 128], jnp.float32(-1.0))
-                downs[c] = jnp.maximum(downs[c], jnp.max(kept.reshape(8, 8, 128), axis=0))
+                down = jnp.max(kept.reshape(8, 8, 128), axis=0)
+                col_best[b * 8 + c] = jnp.maximum(col_best[b * 8 + c], down)
                 best = jnp.maximum(best, kept)
             row_best[unit, first_row:first_row + 64] = best
-        for c in range(2):
-            col_best[a * 8 + 2 * t + c] = downs[c]
 
     def compare(t, j):
         a, b = todo[0], todo[1]
@@ -264,8 +265,16 @@
     def own_pair(t):
         pl.when(h == 1)(lambda: strip(0, t, 0, t + 1, diagonal=True))
 
-    def wait_shared(m):
+    def finish_rows(t):
         for s in range(SLOTS):
+            @pl.when(need[s] == 1)
+            def _():
+                for core in range(2):
+                    unit = s * 8 + 2 * t + core
+                    row_line[unit:unit + 1, :] = jnp.max(row_best[unit].T, axis=0, keepdims=True)
+
+    def wait_shared(m, slots=range(SLOTS)):
+        for s in slots:
             @pl.when(need[s] == 1)
             def _():
                 for half in range(2):
@@ -319,22 +328,24 @@
                 compare(m, j)
             take(k - 3)
         own_pair(m)
+        finish_rows(m)
     for m in (2, 3):
-        wait_shared(m)
-
-        @pl.loop(0, pair_count)
-        def _(j):
-            compare(m, j)
+        wait_shared(m, (0,))
         own_pair(m)
-        if m == 2:
-            take(6)
-            take(7)
-
-    for s in range(SLOTS):
-        @pl.when(need[s] == 1)
-        def _():
-            for unit in range(s * 8, s * 8 + 8):
-                row_line[unit:unit + 1, :] = jnp.max(row_best[unit].T, axis=0, keepdims=True)
+    wait_shared(2, range(1, SLOTS))
+
+    @pl.loop(0, pair_count)
+    def _(j):
+        compare(2, j)
+    take(6)
+    take(7)
+    finish_rows(2)
+    wait_shared(3, range(1, SLOTS))
+
+    @pl.loop(0, pair_count)
+    def _(j):
+        compare(3, j)
+    finish_rows(3)
 
     for s in range(SLOTS):
         for t in range(4):
@@ -356,16 +367,6 @@
             else:
                 copy.start()
 
-    best = None
-    for k in range(2 * SLOTS):
-        got = remote(parts_got.at[k], parts_got.at[k], r_send.at[k], r_recv.at[k], sibling)
-        if k < 2:
-            pl.when(jnp.logical_not(jnp.logical_and(mine, h == k)))(got.wait_recv)
-        else:
-            got.wait_recv()
-        best = parts_got[k] if best is None else jnp.maximum(best, parts_got[k])
-    out[...] = best
-
     ids_copy.wait_send()
     for half in range(2):
         for copy in (swap(1, half), swap(2, half), relay_in(half), relay_out(half)):
@@ -376,6 +377,17 @@
     for s in range(SLOTS):
         for t in range(8):
             pl.when(sibling_need[s] == 1)(lambda s=s, t=t: share(s, t).wait_send())
+    best = None
+    for k in range(2 * SLOTS):
+        got = remote(parts_got.at[k], parts_got.at[k], r_send.at[k], r_recv.at[k], sibling)
+        if k < 2:
+            pl.when(jnp.logical_not(jnp.logical_and(mine, h == k)))(got.wait_recv)
+        else:
+            got.wait_recv()
+        best = parts_got[k] if best is None else jnp.maximum(best, parts_got[k])
+    out[...] = best
+
+    for s in range(SLOTS):
         for half in range(2):
             copy = remote(part.at[s * 2 + half], parts_got.at[place[s] * 2 + h], r_send.at[s * 2 + half],
                           r_recv.at[place[s] * 2 + h], (owner_grp, held[s] * 2 + half))
@@ -392,12 +404,13 @@
     best = pl.pallas_call(
         kernel,
         out_shape=jax.ShapeDtypeStruct((4, 128), jnp.float32),
-        in_specs=[pl.BlockSpec(memory_space=pl.ANY), pl.BlockSpec(memory_space=pltpu.VMEM)],
+        in_specs=[pl.BlockSpec(memory_space=pl.ANY), pl.BlockSpec(memory_space=pl.ANY)],
         out_specs=pl.BlockSpec(memory_space=pltpu.VMEM),
         scratch_shapes=[
             pltpu.VMEM((SLOTS, 1024, D), jnp.bfloat16),
             pltpu.VMEM((3, 128, D), jnp.bfloat16),
             pltpu.VMEM((4, 128, D), jnp.float32),
+            pltpu.VMEM((128, 128), jnp.int32),
             pltpu.VMEM((128, 128), jnp.int32),
             pltpu.VMEM((SLOTS * 8, 128, 128), jnp.float32),
             pltpu.VMEM((128, 128), jnp.float32),
@@ -407,7 +420,7 @@
             pltpu.VMEM((2 * SLOTS, 4, 128), jnp.float32),
             pltpu.VMEM((2 * SLOTS, 4, 128), jnp.float32),
             pltpu.VMEM((128, D), jnp.bfloat16),
-            dma((4,)), dma, dma, dma((3, 2)), dma((3, 2)), dma((2, 2)), dma((2,)), dma((4, STEPS)), dma((4, STEPS)),
+            dma((4,)), dma, dma, dma, dma((3, 2)), dma((3, 2)), dma((2, 2)), dma((2,)), dma((4, STEPS)), dma((4, STEPS)),
             dma((SLOTS, 8)), dma((SLOTS, 8)), dma((2 * SLOTS,)), dma((2 * SLOTS,)),
         ],
         compiler_params=pltpu.CompilerParams(

time: 47.1 us -> 45.1 us (0.958)
  Pallas kernels: 45.6 us -> 43.6 us
    pallas_call x1, Pallas kernels: 45.6 us -> 43.6 us  [on_device(): pl.pallas_call(kernel, out_shape=jax.ShapeDtypeStruct((4, 128), jnp.float...]
where the time goes in v1:
time: 45.1 us; the launch traced here: 44.9 us
  Pallas kernels  43.6 us (97%)
  local copies, waits for them, and re-layouts  1.26 us (3%)
    pallas_call x1, Pallas kernels, on_device(): pl.pallas_call(kernel, out_shape=jax.ShapeDtypeStruct((4, 128), jnp.float...  43.6 us
    unnamed x1, local copies, waits for them, and re-layouts  1.26 us

profile of v1, /device:TPU:1, one launch (start us, length us, event | category | flops | bytes accessed | tf_op | source)
XLA Modules:
  0.0 44.9 jit_solution(7585637254143679118)
XLA Ops:
  0.0 43.6 %best_match.1 = f32[4,128]{1,0:T(4,128)} custom-call(f32[4,128,768]{2,1,0:T(8,128)} %bitcast.4, s32[128,128]{1,0:T(8,128)} %bitcast.5), custom_call_target="tpu_custom_call" | custom-call | flops 7000000000 | bytes 2000000 | tf_op jit(solution)/shard_map/best_match/pallas_call | solution.py:404
  43.6 1.3 %copy.4 = f32[1,512]{1,0:T(1,128)} copy(f32[1,512]{1,0:T(1,128)} %bitcast.3) | data formatting | bytes 4096

commit v2 on v1

--- a/solution.py
+++ b/solution.py
@@ -13,32 +13,39 @@
 PIECE = 64
 STEPS = 8
 
-SRC = [[0, 3, 0, 0], [3, 0, 0, 0], [0, 0, 4, 0], [0, 0, 4, 0], [0, 4, 1, 0], [4, 0, 2, 0], [0, 3, 0, 0], [3, 0, 0, 0],
-       [3, 0, 0, 3], [0, 3, 0, 3], [2, 4, 0, 0], [4, 1, 0, 0], [2, 0, 4, 0], [0, 1, 4, 0], [4, 0, 0, 3], [0, 4, 0, 3]]
-DEP = [[1, 1, 1, 2], [1, 1, 1, 2], [1, 2, 1, 1], [2, 1, 1, 1], [1, 2, 2, 1], [2, 1, 2, 1], [1, 2, 1, 2], [2, 1, 1, 2],
-       [2, 2, 1, 2], [2, 2, 1, 2], [2, 1, 2, 1], [1, 2, 2, 1], [2, 1, 1, 1], [1, 2, 1, 1], [2, 1, 1, 1], [1, 2, 1, 1]]
-BLK = [[1, 3, 4, 8], [2, 0, 5, 9], [3, 5, 6, 14], [4, 2, 7, 15], [5, 11, 12, 0], [10, 4, 13, 1], [7, 1, 10, 14],
-       [0, 6, 11, 15], [13, 7, 12, 5], [6, 12, 13, 4], [8, 9, 2, 6], [8, 9, 3, 7], [14, 15, 0, 8], [14, 15, 1, 9],
-       [11, 13, 2, 10], [12, 10, 3, 11]]
-IDX = [[1, 1, 1, 1], [1, 1, 1, 1], [2, 2, 1, 1], [2, 2, 1, 1], [3, 1, 1, 2], [1, 3, 1, 2], [2, 3, 2, 2], [3, 2, 2, 2],
-       [2, 3, 2, 4], [3, 3, 3, 4], [2, 2, 3, 4], [3, 3, 3, 4], [3, 3, 4, 4], [4, 4, 4, 4], [3, 4, 4, 3], [4, 4, 4, 4]]
-HOLD = [[0, 1, 4, 7, 12], [1, 0, 5, 6, 13], [2, 1, 3, 10, 14], [3, 0, 2, 11, 15], [4, 0, 3, 5, 9], [5, 1, 2, 4, 8],
-        [6, 2, 7, 9, 10], [7, 3, 6, 8, 11], [8, 0, 10, 11, 12], [9, 1, 10, 11, 13], [10, 5, 6, 14, 15], [11, 4, 7, 14, 15],
-        [12, 4, 8, 9, 15], [13, 5, 8, 9, 14], [14, 2, 6, 12, 13], [15, 3, 7, 12, 13]]
-PAIRS = [[[(1, 3), (1, 4), (3, 4)], [(0, 1), (0, 2), (1, 2)]], [[(2, 1), (2, 4), (1, 4)], [(0, 1), (0, 3), (3, 4)]],
-         [[(1, 3), (3, 4), (2, 3), (2, 4)], [(0, 1), (0, 2), (1, 2)]],
-         [[(2, 3), (2, 1), (1, 3)], [(0, 3), (3, 4), (0, 1)]], [[(4, 0), (4, 1), (0, 2), (1, 2)], [(0, 3), (1, 3)]],
-         [[(2, 0), (4, 1), (2, 1)], [(0, 1), (0, 3), (1, 3)]], [[(1, 3), (1, 4), (3, 4)], [(0, 3), (2, 0), (2, 1)]],
-         [[(2, 3), (2, 4), (3, 4)], [(2, 0), (1, 2), (1, 0)]],
-         [[(2, 3), (2, 1), (0, 1), (3, 1)], [(4, 2), (4, 0), (2, 0)]],
-         [[(4, 1), (4, 0), (4, 3), (1, 3)], [(1, 0), (1, 2), (0, 2)]],
-         [[(3, 4), (3, 1), (4, 1)], [(2, 0), (1, 2), (1, 0)]], [[(1, 0), (3, 1), (3, 2)], [(4, 0), (4, 2), (2, 0)]],
-         [[(3, 4), (4, 1), (0, 1)], [(4, 0), (4, 2), (0, 2)]], [[(3, 4), (4, 1), (1, 2)], [(4, 0), (4, 2), (0, 2)]],
-         [[(3, 4), (3, 1), (4, 1)], [(2, 0), (1, 2), (1, 0)]], [[(3, 4), (3, 1), (4, 1)], [(3, 2), (2, 1), (2, 0)]]]
-NEED = [[[1, 3, 4], [0, 1, 2]], [[1, 2, 4], [0, 1, 3, 4]], [[1, 2, 3, 4], [0, 1, 2]], [[1, 2, 3], [0, 1, 3, 4]],
-        [[0, 1, 2, 4], [0, 1, 3]], [[0, 1, 2, 4], [0, 1, 3]], [[1, 3, 4], [0, 1, 2, 3]], [[2, 3, 4], [0, 1, 2]],
-        [[0, 1, 2, 3], [0, 2, 4]], [[0, 1, 3, 4], [0, 1, 2]], [[1, 3, 4], [0, 1, 2]], [[0, 1, 2, 3], [0, 2, 4]],
-        [[0, 1, 3, 4], [0, 2, 4]], [[1, 2, 3, 4], [0, 2, 4]], [[1, 3, 4], [0, 1, 2]], [[1, 3, 4], [0, 1, 2, 3]]]
+SRC = [[4, 0, 0, 2], [0, 4, 0, 1], [0, 0, 0, 2], [0, 0, 0, 1], [4, 0, 0, 2], [0, 4, 0, 1], [0, 0, 1, 2],
+       [0, 0, 2, 1], [4, 0, 0, 0], [0, 4, 0, 0], [0, 1, 0, 3], [2, 0, 0, 3], [4, 0, 0, 0], [0, 4, 0, 0],
+       [0, 0, 4, 0], [0, 0, 4, 0]]
+DEP = [[2, 1, 2, 1], [1, 2, 2, 1], [1, 1, 2, 2], [1, 1, 2, 2], [2, 1, 1, 1], [1, 2, 1, 1], [1, 1, 2, 1],
+       [1, 1, 2, 1], [2, 2, 1, 1], [2, 2, 1, 1], [1, 1, 1, 2], [1, 1, 1, 2], [2, 1, 2, 1], [1, 2, 2, 1],
+       [1, 1, 2, 1], [1, 1, 2, 1]]
+BLK = [[13, 3, 7, 12], [2, 12, 6, 13], [3, 1, 5, 10], [0, 2, 4, 11], [1, 7, 8, 0], [6, 0, 9, 1], [7, 5, 14, 2],
+       [4, 6, 15, 3], [5, 10, 12, 4], [11, 4, 13, 5], [11, 9, 14, 7], [8, 10, 15, 6], [9, 15, 3, 8], [14, 8, 2, 9],
+       [15, 13, 1, 10], [12, 14, 0, 11]]
+IDX = [[1, 1, 1, 1], [1, 2, 1, 2], [2, 1, 1, 1], [1, 2, 1, 1], [2, 2, 1, 2], [2, 3, 1, 3], [3, 2, 1, 3],
+       [2, 3, 1, 3], [3, 2, 3, 3], [2, 4, 3, 4], [3, 2, 2, 4], [2, 3, 2, 4], [3, 3, 4, 3], [3, 4, 4, 4],
+       [4, 4, 4, 4], [4, 4, 4, 4]]
+HOLD = [[0, 3, 4, 5, 15], [1, 2, 4, 5, 14], [2, 1, 3, 6, 13], [3, 0, 2, 7, 12], [4, 3, 7, 8, 9], [5, 2, 6, 8, 9],
+        [6, 1, 5, 7, 11], [7, 0, 4, 6, 10], [8, 4, 11, 12, 13], [9, 5, 10, 12, 13], [10, 2, 8, 11, 14],
+        [11, 3, 9, 10, 15], [12, 0, 1, 8, 15], [13, 0, 1, 9, 14], [14, 6, 10, 13, 15], [15, 7, 11, 12, 14]]
+PAIRS = [[[(2, 4), (3, 4), (3, 1)], [(0, 2), (0, 3), (2, 3)]], [[(3, 2), (3, 4), (2, 4)], [(0, 1), (1, 3), (0, 3)]],
+         [[(2, 1), (1, 3), (2, 3)], [(0, 4), (1, 4), (3, 4)]], [[(1, 2), (2, 3), (3, 4)], [(2, 0), (2, 4), (0, 4)]],
+         [[(2, 3), (1, 2), (1, 3)], [(4, 3), (4, 0), (1, 0), (4, 1)]],
+         [[(1, 3), (2, 1), (2, 3)], [(4, 3), (0, 3), (2, 0)]],
+         [[(4, 1), (4, 2), (2, 3)], [(2, 1), (0, 1), (2, 0), (0, 3)]],
+         [[(4, 2), (1, 2), (2, 3)], [(4, 1), (1, 0), (0, 3)]],
+         [[(4, 3), (4, 2), (2, 3)], [(4, 0), (1, 0), (1, 3), (4, 1)]],
+         [[(4, 3), (4, 1), (1, 3)], [(0, 3), (2, 0), (2, 3)]], [[(2, 1), (4, 2), (4, 1)], [(2, 0), (4, 0), (4, 3)]],
+         [[(1, 0), (4, 1), (4, 0)], [(1, 2), (2, 0), (4, 2)]], [[(4, 2), (3, 4), (3, 1)], [(4, 0), (1, 0), (1, 2)]],
+         [[(3, 2), (3, 4), (2, 4)], [(4, 1), (2, 0), (2, 1)]], [[(4, 2), (2, 1), (4, 1)], [(4, 0), (2, 0), (3, 4)]],
+         [[(4, 1), (1, 2), (4, 2)], [(1, 0), (2, 0), (4, 0)]]]
+EARLY = [[1, 1], [0, 1], [1, 0], [1, 1], [1, 2], [1, 2], [2, 3], [2, 2], [1, 1], [1, 1], [1, 1], [1, 2], [1, 1],
+         [0, 1], [3, 2], [3, 3]]
+NEED = [[[1, 2, 3, 4], [0, 2, 3]], [[2, 3, 4], [0, 1, 3]], [[1, 2, 3], [0, 1, 3, 4]], [[1, 2, 3, 4], [0, 2, 4]],
+        [[1, 2, 3], [0, 1, 3, 4]], [[1, 2, 3], [0, 2, 3, 4]], [[1, 2, 3, 4], [0, 1, 2, 3]],
+        [[1, 2, 3, 4], [0, 1, 3, 4]], [[2, 3, 4], [0, 1, 3, 4]], [[1, 3, 4], [0, 2, 3]], [[1, 2, 4], [0, 2, 3, 4]],
+        [[0, 1, 4], [0, 1, 2, 4]], [[1, 2, 3, 4], [0, 1, 2, 4]], [[2, 3, 4], [0, 1, 2, 4]],
+        [[1, 2, 4], [0, 2, 3, 4]], [[1, 2, 4], [0, 1, 2, 4]]]
 
 REL = (0, 3, 1, 2)
 
@@ -92,10 +99,10 @@
     for c in range(16):
         for core in range(2):
             flat = [slot for pair in PAIRS[c][core] for slot in pair]
-            lists.append(len(PAIRS[c][core]) + 8 * word(flat + [0] * (8 - len(flat)), 8))
+            lists.append(len(PAIRS[c][core]) + 8 * EARLY[c][core] + 64 * word(flat + [0] * (8 - len(flat)), 8))
     todo = look_up(p * 2 + h, lists)
-    pair_count = todo % 8
-    todo = digits_of(todo // 8, 8, 8)
+    pair_count, early_count = todo % 8, todo // 8 % 8
+    todo = digits_of(todo // 64, 8, 8)
 
     needs = [[sum(1 << slot for slot in NEED[c][core]) for core in range(2)] for c in range(16)]
     need = digits_of(look_up(p * 2 + h, [needs[c][core] for c in range(16) for core in range(2)]), 2, SLOTS)
@@ -273,9 +280,18 @@
                     unit = s * 8 + 2 * t + core
                     row_line[unit:unit + 1, :] = jnp.max(row_best[unit].T, axis=0, keepdims=True)
 
-    def wait_shared(m, slots=range(SLOTS)):
-        for s in slots:
-            @pl.when(need[s] == 1)
+    def wait_shared(m, links):
+        for s in range(SLOTS):
+            there = need[s] == 1
+            if s == 0:
+                if links:
+                    continue
+            elif links:
+                there = jnp.logical_and(there, dep[s - 1] == links)
+            else:
+                continue
+
+            @pl.when(there)
             def _():
                 for half in range(2):
                     shared(s, 2 * m + half).wait_recv()
@@ -310,41 +326,48 @@
     take(0)
     pass_on(4)
     take(1)
-    for m in range(2):
-        @pl.loop(5 + 2 * m, 7 + 2 * m)
-        def _(k):
-            pass_on(k)
-
-            @pl.when(k == 5)
-            def _():
-                for half in range(2):
-                    relay_out(half).wait_recv()
-                    own_piece_ready(6 + half)
-            first = 2 * (k - 5 - 2 * m)
-            pl.when(first == 0)(lambda: wait_shared(m))
-
-            @pl.loop(first, jnp.minimum(first + 2, pair_count))
-            def _(j):
-                compare(m, j)
-            take(k - 3)
-        own_pair(m)
-        finish_rows(m)
-    for m in (2, 3):
-        wait_shared(m, (0,))
-        own_pair(m)
-    wait_shared(2, range(1, SLOTS))
+    pass_on(5)
+    for half in range(2):
+        relay_out(half).wait_recv()
+        own_piece_ready(6 + half)
+    wait_shared(0, 0)
+    wait_shared(0, 1)
+    wait_shared(0, 2)
 
     @pl.loop(0, pair_count)
     def _(j):
-        compare(2, j)
-    take(6)
-    take(7)
-    finish_rows(2)
-    wait_shared(3, range(1, SLOTS))
+        compare(0, j)
+    own_pair(0)
+    take(2)
+    pass_on(6)
+    for m in (1, 2, 3):
+        wait_shared(m, 0)
+        own_pair(m)
+    finish_rows(0)
+    take(3)
+    pass_on(7)
+    wait_shared(1, 1)
+    wait_shared(1, 2)
 
     @pl.loop(0, pair_count)
     def _(j):
-        compare(3, j)
+        compare(1, j)
+    take(4)
+    pass_on(8)
+    take(5)
+
+    for m in (2, 3):
+        wait_shared(m, 1)
+
+        @pl.loop(0, pair_count)
+        def _(j):
+            pl.when(j == early_count)(lambda: wait_shared(m, 2))
+            compare(m, j)
+        if m == 2:
+            finish_rows(1)
+            take(6)
+            finish_rows(2)
+            take(7)
     finish_rows(3)
 
     for s in range(SLOTS):

time: 45.1 us -> 45.9 us (1.018)
  Pallas kernels: 43.6 us -> 44.5 us
    pallas_call x1, Pallas kernels: 43.6 us -> 44.5 us  [on_device(): pl.pallas_call(kernel, out_shape=jax.ShapeDtypeStruct((4, 128), jnp.float...]
where the time goes in v2:
time: 45.9 us; the launch traced here: 45.7 us
  Pallas kernels  44.5 us (97%)
  local copies, waits for them, and re-layouts  1.26 us (3%)
    pallas_call x1, Pallas kernels, on_device(): pl.pallas_call(kernel, out_shape=jax.ShapeDtypeStruct((4, 128), jnp.float...  44.5 us
    unnamed x1, local copies, waits for them, and re-layouts  1.26 us

profile of v2, /device:TPU:1, one launch (start us, length us, event | category | flops | bytes accessed | tf_op | source)
XLA Modules:
  0.0 45.7 jit_solution(8871970348070615893)
XLA Ops:
  0.0 44.5 %best_match.1 = f32[4,128]{1,0:T(4,128)} custom-call(f32[4,128,768]{2,1,0:T(8,128)} %bitcast.4, s32[128,128]{1,0:T(8,128)} %bitcast.5), custom_call_target="tpu_custom_call" | custom-call | flops 7000000000 | bytes 2000000 | tf_op jit(solution)/shard_map/best_match/pallas_call | solution.py:427
  44.5 1.3 %copy.4 = f32[1,512]{1,0:T(1,128)} copy(f32[1,512]{1,0:T(1,128)} %bitcast.3) | data formatting | bytes 4096

commit v3 on v2

--- a/solution.py
+++ b/solution.py
@@ -323,38 +323,44 @@
         relay_out(half).start()
     swap(2, 1).wait_recv()
     own_piece_ready(5)
+    wait_shared(0, 0)
+    own_pair(0)
     take(0)
     pass_on(4)
+    wait_shared(1, 0)
+    own_pair(1)
     take(1)
     pass_on(5)
     for half in range(2):
         relay_out(half).wait_recv()
         own_piece_ready(6 + half)
-    wait_shared(0, 0)
     wait_shared(0, 1)
     wait_shared(0, 2)
 
     @pl.loop(0, pair_count)
     def _(j):
         compare(0, j)
-    own_pair(0)
     take(2)
     pass_on(6)
-    for m in (1, 2, 3):
+    for m in (2, 3):
         wait_shared(m, 0)
         own_pair(m)
+    take(3)
+
+    @pl.loop(0, 2)
+    def _(k):
+        pass_on(7 + k)
+
+        @pl.when(k == 0)
+        def _():
+            wait_shared(1, 1)
+            wait_shared(1, 2)
+
+        @pl.loop(2 * k, jnp.minimum(2 * k + 2, pair_count))
+        def _(j):
+            compare(1, j)
+        take(4 + k)
     finish_rows(0)
-    take(3)
-    pass_on(7)
-    wait_shared(1, 1)
-    wait_shared(1, 2)
-
-    @pl.loop(0, pair_count)
-    def _(j):
-        compare(1, j)
-    take(4)
-    pass_on(8)
-    take(5)
 
     for m in (2, 3):
         wait_shared(m, 1)
@@ -447,7 +453,7 @@
             dma((SLOTS, 8)), dma((SLOTS, 8)), dma((2 * SLOTS,)), dma((2 * SLOTS,)),
         ],
         compiler_params=pltpu.CompilerParams(
-            collective_id=0, has_side_effects=True, vmem_limit_bytes=60 * 1024 * 1024),
+            collective_id=0, has_side_effects=True, vmem_limit_bytes=55168 * 1024),
         cost_estimate=pl.CostEstimate(flops=7 * 10**9, bytes_accessed=2 * 10**6, transcendentals=0),
         name="best_match",
     )(emb, ids)

time: 45.9 us -> 44.5 us (0.969)
  Pallas kernels: 44.5 us -> 43.8 us
  local copies, waits for them, and re-layouts: 1.26 us -> 0.58 us
    pallas_call x1, Pallas kernels: 44.5 us -> 43.8 us  [on_device(): pl.pallas_call(kernel, out_shape=jax.ShapeDtypeStruct((4, 128), jnp.float...]
    unnamed x1, local copies, waits for them, and re-layouts: 1.26 us -> 0.58 us
where the time goes in v3:
time: 44.5 us; the launch traced here: 44.4 us
  Pallas kernels  43.8 us (98%)
  local copies, waits for them, and re-layouts  0.58 us (1%)
    pallas_call x1, Pallas kernels, on_device(): pl.pallas_call(kernel, out_shape=jax.ShapeDtypeStruct((4, 128), jnp.float...  43.8 us

profile of v3, /device:TPU:1, one launch (start us, length us, event | category | flops | bytes accessed | tf_op | source)
XLA Modules:
  0.0 44.4 jit_solution(12242736946367847928)
XLA Ops:
  0.0 43.8 %best_match.1 = f32[4,128]{1,0:T(4,128)S(1)} custom-call(f32[4,128,768]{2,1,0:T(8,128)} %bitcast.4, s32[128,128]{1,0:T(8,128)} %bitcast.5), custom_call_target="tpu_custom_call" | custom-call | flops 7000000000 | bytes 2000000 | tf_op jit(solution)/shard_map/best_match/pallas_call | solution.py:433
  43.8 0.6 %copy.4 = f32[1,512]{1,0:T(1,128)} copy(f32[1,512]{1,0:T(1,128)S(1)} %bitcast.3) | data formatting | bytes 4096

commit v4 on v3

--- a/solution.py
+++ b/solution.py
@@ -72,6 +72,13 @@
     return out
 
 
+def pick(values, index):
+    got = values[0]
+    for k in range(1, len(values)):
+        got = jnp.where(index == k, values[k], got)
+    return got
+
+
 def kernel(emb, ids_in, out, x, units, stage, ids_own, ids_got, ids_rows, ids_cols, row_best, col_best, row_line, part, parts_got,
            relay,
            load_sem, ids_sem, id_send, id_recv, z_send, z_recv, relay_send, relay_recv, f_send, f_recv, c_send, c_recv, r_send, r_recv):
@@ -241,20 +248,20 @@
     for j in range(SLOTS * 8):
         ids_rows[j] = jnp.broadcast_to(turned[:, j:j + 1], (128, 128))
 
-    def strip(a, t, b, count, diagonal=False):
-        sim = lax.dot_general(x[a, 256 * t:256 * t + 256, :], x[b, 0:256 * count, :], (((1,), (1,)), ((), ())),
+    def strip(a, t, b, count, diagonal=False, first=0):
+        sim = lax.dot_general(x[a, 256 * t:256 * t + 256, :], x[b, 256 * first:256 * count, :], (((1,), (1,)), ((), ())),
                               preferred_element_type=jnp.float32)
         for r in range(4):
             unit, first_row = a * 8 + 2 * t + r // 2, 64 * (r % 2)
             row_ids = ids_rows[unit, first_row:first_row + 64]
             best = row_best[unit, first_row:first_row + 64]
-            for c in range(2 * count):
+            for c in range(2 * first, 2 * count):
                 keep = row_ids == ids_cols[pl.ds(b * 8 + c, 1), :]
                 if diagonal and c // 2 == t:
                     row = lax.broadcasted_iota(jnp.int32, (64, 128), 0) + 64 * r
                     col = lax.broadcasted_iota(jnp.int32, (64, 128), 1) + 128 * (c % 2)
                     keep = jnp.logical_and(keep, row != col)
-                kept = jnp.where(keep, sim[64 * r:64 * r + 64, 128 * c:128 * c + 128], jnp.float32(-1.0))
+                kept = jnp.where(keep, sim[64 * r:64 * r + 64, 128 * (c - 2 * first):128 * (c - 2 * first) + 128], jnp.float32(-1.0))
                 down = jnp.max(kept.reshape(8, 8, 128), axis=0)
                 col_best[b * 8 + c] = jnp.maximum(col_best[b * 8 + c], down)
                 best = jnp.maximum(best, kept)
@@ -269,16 +276,42 @@
         if t:
             strip(b, t, a, t)
 
+    def pair(j):
+        return pick(todo[0:8:2], j), pick(todo[1:8:2], j)
+
+    def half_strip(a, core, b):
+        unit = a * 8 + 6 + core
+        sim = lax.dot_general(x[a, pl.ds(pl.multiple_of(768 + 128 * core, 128), 128), :], x[b, 0:768, :],
+                              (((1,), (1,)), ((), ())), preferred_element_type=jnp.float32)
+        for r in range(2):
+            rows = slice(64 * r, 64 * r + 64)
+            best = row_best[unit, rows]
+            for c in range(6):
+                keep = ids_rows[unit, rows] == ids_cols[pl.ds(b * 8 + c, 1), :]
+                kept = jnp.where(keep, sim[rows, 128 * c:128 * c + 128], jnp.float32(-1.0))
+                col_best[b * 8 + c] = jnp.maximum(col_best[b * 8 + c], jnp.max(kept.reshape(8, 8, 128), axis=0))
+                best = jnp.maximum(best, kept)
+            row_best[unit, rows] = best
+
+    def compare_here(j):
+        a, b = pair(j)
+        half_strip(a, h, b)
+        half_strip(b, h, a)
+
+    def compare_there(j):
+        a, b = pair(j)
+        half_strip(a, 1 - h, b)
+        half_strip(b, 1 - h, a)
+        strip(a, 3, b, 4, first=3)
+
     def own_pair(t):
         pl.when(h == 1)(lambda: strip(0, t, 0, t + 1, diagonal=True))
 
     def finish_rows(t):
         for s in range(SLOTS):
-            @pl.when(need[s] == 1)
-            def _():
-                for core in range(2):
-                    unit = s * 8 + 2 * t + core
-                    row_line[unit:unit + 1, :] = jnp.max(row_best[unit].T, axis=0, keepdims=True)
+            for core in range(2):
+                unit = s * 8 + 2 * t + core
+                row_line[unit:unit + 1, :] = jnp.max(row_best[unit].T, axis=0, keepdims=True)
 
     def wait_shared(m, links):
         for s in range(SLOTS):
@@ -362,18 +395,30 @@
         take(4 + k)
     finish_rows(0)
 
-    for m in (2, 3):
-        wait_shared(m, 1)
-
-        @pl.loop(0, pair_count)
-        def _(j):
-            pl.when(j == early_count)(lambda: wait_shared(m, 2))
-            compare(m, j)
-        if m == 2:
-            finish_rows(1)
-            take(6)
-            finish_rows(2)
-            take(7)
+    wait_shared(2, 1)
+
+    @pl.loop(0, pair_count)
+    def _(j):
+        pl.when(j == early_count)(lambda: wait_shared(2, 2))
+        compare(2, j)
+    finish_rows(1)
+    take(6)
+    finish_rows(2)
+    take(7)
+    wait_shared(3, 1)
+
+    @pl.loop(0, early_count)
+    def _(j):
+        compare(3, j)
+
+    @pl.loop(early_count, pair_count)
+    def _(j):
+        compare_here(j)
+    wait_shared(3, 2)
+
+    @pl.loop(early_count, pair_count)
+    def _(j):
+        compare_there(j)
     finish_rows(3)
 
     for s in range(SLOTS):

time: 44.5 us -> 45.1 us (1.013)
  no operation moved by 1% of the time
where the time goes in v4:
time: 45.1 us; the launch traced here: 44.7 us
  Pallas kernels  44.2 us (98%)
  local copies, waits for them, and re-layouts  0.58 us (1%)
    pallas_call x1, Pallas kernels, on_device(): pl.pallas_call(kernel, out_shape=jax.ShapeDtypeStruct((4, 128), jnp.float...  44.2 us

profile of v4, /device:TPU:1, one launch (start us, length us, event | category | flops | bytes accessed | tf_op | source)
XLA Modules:
  0.0 44.7 jit_solution(17978703038325085278)
XLA Ops:
  0.0 44.2 %best_match.1 = f32[4,128]{1,0:T(4,128)S(1)} custom-call(f32[4,128,768]{2,1,0:T(8,128)} %bitcast.4, s32[128,128]{1,0:T(8,128)} %bitcast.5), custom_call_target="tpu_custom_call" | custom-call | flops 7000000000 | bytes 2000000 | tf_op jit(solution)/shard_map/best_match/pallas_call | solution.py:478
  44.2 0.6 %copy.4 = f32[1,512]{1,0:T(1,128)} copy(f32[1,512]{1,0:T(1,128)S(1)} %bitcast.3) | data formatting | bytes 4096

commit v5 on v3

--- a/solution.py
+++ b/solution.py
@@ -72,6 +72,13 @@
     return out
 
 
+def pick(values, index):
+    got = values[0]
+    for k in range(1, len(values)):
+        got = jnp.where(index == k, values[k], got)
+    return got
+
+
 def kernel(emb, ids_in, out, x, units, stage, ids_own, ids_got, ids_rows, ids_cols, row_best, col_best, row_line, part, parts_got,
            relay,
            load_sem, ids_sem, id_send, id_recv, z_send, z_recv, relay_send, relay_recv, f_send, f_recv, c_send, c_recv, r_send, r_recv):
@@ -112,11 +119,11 @@
     owner_grp = zl * 2 + zh
     mine = h == zh
 
-    loads = []
-    for k, rel in enumerate((0, 1, 3, 2)):
-        loads.append(pltpu.make_async_copy(emb.at[group_of((z + rel) % 4)], stage.at[k], load_sem.at[k]))
-        loads[-1].start()
-
+    def load(k):
+        return pltpu.make_async_copy(emb.at[group_of((z + pick((0, 1, 3, 2), k)) % 4)], stage.at[k], load_sem.at[k])
+
+    for k in range(4):
+        load(k).start()
     ids_load = pltpu.make_async_copy(ids_in, ids_own, ids_sem)
     ids_load.start()
 
@@ -136,14 +143,14 @@
             else:
                 tell()
 
-    def normalise(k):
-        loads[k].wait()
+    def normalised(k):
         v = stage[k]
         total = jnp.sum(v * v, axis=-1, keepdims=True)
         return (v / jnp.sqrt(total + 1e-06)).astype(jnp.bfloat16)
 
+    load(0).wait()
     own_rows = pl.multiple_of(h * 128, 128)
-    x[0, pl.ds(own_rows, 128), :] = normalise(0)
+    x[0, pl.ds(own_rows, 128), :] = normalised(0)
     pl.semaphore_wait(barrier, jnp.where(mine, 16, 17))
 
     def remote(src_ref, dst_ref, send_sem, recv_sem, to):
@@ -166,7 +173,7 @@
     def swap(k, half):
         rows = pl.ds(pl.multiple_of(k * 256 + h * 128 + half * 64, 64), 64)
         return remote(units.at[k - 1, pl.ds(half * 64, 64), :], x.at[0, rows, :], z_send.at[k - 1, half],
-                      z_recv.at[k - 1, half], device((z + (1, 3, 2)[k - 1]) % 4, h, p))
+                      z_recv.at[k - 1, half], device((z + pick((1, 3), k - 1)) % 4, h, p))
 
     between = device((z + jnp.where(h == 0, 1, 3)) % 4, h, p)
 
@@ -211,36 +218,18 @@
 
     for t in range(2):
         send_own(t)
-    units[0] = normalise(1)
-    for half in range(2):
-        swap(1, half).start()
-    units[1] = normalise(2)
-    for half in range(2):
-        swap(2, half).start()
-    units[2] = normalise(3)
-    for half in range(2):
-        relay_in(half).start()
+    @pl.loop(1, 4)
+    def _(k):
+        load(k).wait()
+        units[k - 1] = normalised(k)
+        for half in range(2):
+            pl.when(k < 3)(lambda half=half: swap(k, half).start())
+            pl.when(k == 3)(lambda half=half: relay_in(half).start())
+
     ids_copy = remote(ids_in, ids_got, id_send, id_recv, sibling)
     ids_copy.start()
     give(0, 0)
     give(0, 1)
-    row_best[...] = jnp.full_like(row_best, -1.0)
-    col_best[...] = jnp.full_like(col_best, -1.0)
-    row_line[...] = jnp.full_like(row_line, -1.0)
-
-    ids_load.wait()
-    ids_copy.wait_recv()
-    ids_cols[...] = jnp.zeros_like(ids_cols)
-    for s in range(SLOTS):
-        for t in range(4):
-            for core in range(2):
-                unit = held[s] * 8 + 2 * ((z + REL[t]) % 4) + core
-                got = jnp.where(mine, ids_own[pl.ds(unit, 1), :], ids_got[pl.ds(unit, 1), :])
-                ids_cols[pl.ds(s * 8 + 2 * t + core, 1), :] = got.astype(jnp.float32)
-    turned = ids_cols[...].T
-    for j in range(SLOTS * 8):
-        ids_rows[j] = jnp.broadcast_to(turned[:, j:j + 1], (128, 128))
-
     def strip(a, t, b, count, diagonal=False):
         sim = lax.dot_general(x[a, 256 * t:256 * t + 256, :], x[b, 0:256 * count, :], (((1,), (1,)), ((), ())),
                               preferred_element_type=jnp.float32)
@@ -317,18 +306,37 @@
     own_piece_ready(3)
     swap(2, 0).wait_recv()
     own_piece_ready(4)
+
+    ids_load.wait()
+    ids_copy.wait_recv()
+    ids_cols[...] = jnp.zeros_like(ids_cols)
+    for s in range(SLOTS):
+        for t in range(4):
+            for core in range(2):
+                unit = held[s] * 8 + 2 * ((z + REL[t]) % 4) + core
+                got = jnp.where(mine, ids_own[pl.ds(unit, 1), :], ids_got[pl.ds(unit, 1), :])
+                ids_cols[pl.ds(s * 8 + 2 * t + core, 1), :] = got.astype(jnp.float32)
+    turned = ids_cols[...].T
+    for j in range(SLOTS * 8):
+        ids_rows[j] = jnp.broadcast_to(turned[:, j:j + 1], (128, 128))
+
     pass_on(3)
     for half in range(2):
         relay_in(half).wait_recv()
         relay_out(half).start()
     swap(2, 1).wait_recv()
     own_piece_ready(5)
-    wait_shared(0, 0)
-    own_pair(0)
+    @pl.loop(0, SLOTS * 8)
+    def _(j):
+        row_best[j] = jnp.full((128, 128), -1.0, jnp.float32)
+        col_best[j] = jnp.full((8, 128), -1.0, jnp.float32)
+    row_line[...] = jnp.full_like(row_line, -1.0)
+
     take(0)
     pass_on(4)
-    wait_shared(1, 0)
-    own_pair(1)
+    for m in (0, 1):
+        wait_shared(m, 0)
+        own_pair(m)
     take(1)
     pass_on(5)
     for half in range(2):
@@ -400,12 +408,14 @@
     for half in range(2):
         for copy in (swap(1, half), swap(2, half), relay_in(half), relay_out(half)):
             copy.wait_send()
-    for d in range(4):
-        for t in range(STEPS):
+
+    @pl.loop(0, STEPS)
+    def _(t):
+        for d in range(4):
             forward(d, t).wait_send()
-    for s in range(SLOTS):
-        for t in range(8):
-            pl.when(sibling_need[s] == 1)(lambda s=s, t=t: share(s, t).wait_send())
+        for s in range(SLOTS):
+            pl.when(sibling_need[s] == 1)(lambda s=s: share(s, t).wait_send())
+
     best = None
     for k in range(2 * SLOTS):
         got = remote(parts_got.at[k], parts_got.at[k], r_send.at[k], r_recv.at[k], sibling)

time: 44.5 us -> 44.5 us (level)
  no operation moved by 1% of the time
where the time goes in v5:
time: 44.5 us; the launch traced here: 44.4 us
  Pallas kernels  43.8 us (98%)
  local copies, waits for them, and re-layouts  0.58 us (1%)
    pallas_call x1, Pallas kernels, on_device(): pl.pallas_call(kernel, out_shape=jax.ShapeDtypeStruct((4, 128), jnp.float...  43.8 us

profile of v5, /device:TPU:1, one launch (start us, length us, event | category | flops | bytes accessed | tf_op | source)
XLA Modules:
  0.0 44.4 jit_solution(6561645030309244670)
XLA Ops:
  0.0 43.8 %best_match.1 = f32[4,128]{1,0:T(4,128)S(1)} custom-call(f32[4,128,768]{2,1,0:T(8,128)} %bitcast.4, s32[128,128]{1,0:T(8,128)} %bitcast.5), custom_call_target="tpu_custom_call" | custom-call | flops 7000000000 | bytes 2000000 | tf_op jit(solution)/shard_map/best_match/pallas_call | solution.py:443
  43.8 0.6 %copy.4 = f32[1,512]{1,0:T(1,128)} copy(f32[1,512]{1,0:T(1,128)S(1)} %bitcast.3) | data formatting | bytes 4096

commit v6 on v5

--- a/solution.py
+++ b/solution.py
@@ -79,9 +79,9 @@
     return got
 
 
-def kernel(emb, ids_in, out, x, units, stage, ids_own, ids_got, ids_rows, ids_cols, row_best, col_best, row_line, part, parts_got,
+def kernel(emb, ids_in, out, x, units, stage, ids_got, ids_rows, ids_cols, row_best, col_best, row_line, part, parts_got,
            relay,
-           load_sem, ids_sem, id_send, id_recv, z_send, z_recv, relay_send, relay_recv, f_send, f_recv, c_send, c_recv, r_send, r_recv):
+           load_sem, id_send, id_recv, z_send, z_recv, relay_send, relay_recv, f_send, f_recv, c_send, c_recv, r_send, r_recv):
     grp, blk = lax.axis_index("grp"), lax.axis_index("blk")
     h, zl = grp % 2, grp // 2
     p, zh = blk // 2, blk % 2
@@ -92,7 +92,7 @@
         return ((z_of % 2) * 2 + core, chip * 2 + z_of // 2)
 
     def group_of(z_of):
-        return (z_of % 2) * 2 + z_of // 2
+        return (1 - z_of % 2) * 2 + z_of // 2
 
     near = [py * 4 + (px + 1) % 4, py * 4 + (px + 3) % 4, ((py + 1) % 4) * 4 + px, ((py + 3) % 4) * 4 + px]
     first = look_up(p, [word(SRC[c], 8) + 4096 * word(DEP[c], 4) for c in range(16)])
@@ -116,32 +116,25 @@
     sibling_need = digits_of(look_up(p * 2 + h, [needs[c][1 - core] for c in range(16) for core in range(2)]), 2, SLOTS)
 
     sibling = device(z, 1 - h, p)
-    owner_grp = zl * 2 + zh
-    mine = h == zh
+    owner_grp = group_of(z)
+    from_z = 2 * h + 1 - zl
+    ids_from = device(2 * h + 1 - zl, zh, p)
 
     def load(k):
         return pltpu.make_async_copy(emb.at[group_of((z + pick((0, 1, 3, 2), k)) % 4)], stage.at[k], load_sem.at[k])
 
     for k in range(4):
         load(k).start()
-    ids_load = pltpu.make_async_copy(ids_in, ids_own, ids_sem)
-    ids_load.start()
-
     barrier = pltpu.get_barrier_semaphore()
     for rel in (1, 3):
         pl.semaphore_signal(barrier, inc=1, device_id=device((z + rel) % 4, h, p), device_id_type=MESH)
     for d in range(4):
         pl.semaphore_signal(barrier, inc=1, device_id=device(z, h, near[d]), device_id_type=MESH)
     pl.semaphore_signal(barrier, inc=1, device_id=sibling, device_id_type=MESH)
-    from_z = 2 * h + zl
+    pl.semaphore_signal(barrier, inc=1, device_id=ids_from, device_id_type=MESH)
     for k in range(SLOTS):
         for core in range(2):
-            def tell():
-                pl.semaphore_signal(barrier, inc=1, device_id=device(from_z, core, holders[k]), device_id_type=MESH)
-            if k == 0:
-                pl.when(jnp.logical_not(jnp.logical_and(mine, h == core)))(tell)
-            else:
-                tell()
+            pl.semaphore_signal(barrier, inc=1, device_id=device(from_z, core, holders[k]), device_id_type=MESH)
 
     def normalised(k):
         v = stage[k]
@@ -151,7 +144,7 @@
     load(0).wait()
     own_rows = pl.multiple_of(h * 128, 128)
     x[0, pl.ds(own_rows, 128), :] = normalised(0)
-    pl.semaphore_wait(barrier, jnp.where(mine, 16, 17))
+    pl.semaphore_wait(barrier, 18)
 
     def remote(src_ref, dst_ref, send_sem, recv_sem, to):
         return pltpu.make_async_remote_copy(
@@ -226,7 +219,7 @@
             pl.when(k < 3)(lambda half=half: swap(k, half).start())
             pl.when(k == 3)(lambda half=half: relay_in(half).start())
 
-    ids_copy = remote(ids_in, ids_got, id_send, id_recv, sibling)
+    ids_copy = remote(ids_in, ids_got, id_send, id_recv, device(from_z, zh, p))
     ids_copy.start()
     give(0, 0)
     give(0, 1)
@@ -307,15 +300,13 @@
     swap(2, 0).wait_recv()
     own_piece_ready(4)
 
-    ids_load.wait()
     ids_copy.wait_recv()
     ids_cols[...] = jnp.zeros_like(ids_cols)
     for s in range(SLOTS):
         for t in range(4):
             for core in range(2):
                 unit = held[s] * 8 + 2 * ((z + REL[t]) % 4) + core
-                got = jnp.where(mine, ids_own[pl.ds(unit, 1), :], ids_got[pl.ds(unit, 1), :])
-                ids_cols[pl.ds(s * 8 + 2 * t + core, 1), :] = got.astype(jnp.float32)
+                ids_cols[pl.ds(s * 8 + 2 * t + core, 1), :] = ids_got[pl.ds(unit, 1), :].astype(jnp.float32)
     turned = ids_cols[...].T
     for j in range(SLOTS * 8):
         ids_rows[j] = jnp.broadcast_to(turned[:, j:j + 1], (128, 128))
@@ -394,15 +385,7 @@
         for half in range(2):
             copy = remote(part.at[s * 2 + half], parts_got.at[place[s] * 2 + h], r_send.at[s * 2 + half],
                           r_recv.at[place[s] * 2 + h], (owner_grp, held[s] * 2 + half))
-            if s == 0:
-                keep_it = jnp.logical_and(mine, zh == half)
-                pl.when(jnp.logical_not(keep_it))(copy.start)
-
-                @pl.when(keep_it)
-                def _():
-                    parts_got[h] = part[half]
-            else:
-                copy.start()
+            copy.start()
 
     ids_copy.wait_send()
     for half in range(2):
@@ -419,10 +402,7 @@
     best = None
     for k in range(2 * SLOTS):
         got = remote(parts_got.at[k], parts_got.at[k], r_send.at[k], r_recv.at[k], sibling)
-        if k < 2:
-            pl.when(jnp.logical_not(jnp.logical_and(mine, h == k)))(got.wait_recv)
-        else:
-            got.wait_recv()
+        got.wait_recv()
         best = parts_got[k] if best is None else jnp.maximum(best, parts_got[k])
     out[...] = best
 
@@ -430,10 +410,7 @@
         for half in range(2):
             copy = remote(part.at[s * 2 + half], parts_got.at[place[s] * 2 + h], r_send.at[s * 2 + half],
                           r_recv.at[place[s] * 2 + h], (owner_grp, held[s] * 2 + half))
-            if s == 0:
-                pl.when(jnp.logical_not(jnp.logical_and(mine, zh == half)))(copy.wait_send)
-            else:
-                copy.wait_send()
+            copy.wait_send()
 
 
 def on_device(embeddings, cluster_ids):
@@ -450,7 +427,6 @@
             pltpu.VMEM((3, 128, D), jnp.bfloat16),
             pltpu.VMEM((4, 128, D), jnp.float32),
             pltpu.VMEM((128, 128), jnp.int32),
-            pltpu.VMEM((128, 128), jnp.int32),
             pltpu.VMEM((SLOTS * 8, 128, 128), jnp.float32),
             pltpu.VMEM((128, 128), jnp.float32),
             pltpu.VMEM((SLOTS * 8, 128, 128), jnp.float32),
@@ -459,7 +435,7 @@
             pltpu.VMEM((2 * SLOTS, 4, 128), jnp.float32),
             pltpu.VMEM((2 * SLOTS, 4, 128), jnp.float32),
             pltpu.VMEM((128, D), jnp.bfloat16),
-            dma((4,)), dma, dma, dma, dma((3, 2)), dma((3, 2)), dma((2, 2)), dma((2,)), dma((4, STEPS)), dma((4, STEPS)),
+            dma((4,)), dma, dma, dma((3, 2)), dma((3, 2)), dma((2, 2)), dma((2,)), dma((4, STEPS)), dma((4, STEPS)),
             dma((SLOTS, 8)), dma((SLOTS, 8)), dma((2 * SLOTS,)), dma((2 * SLOTS,)),
         ],
         compiler_params=pltpu.CompilerParams(

time: 44.5 us -> 43.6 us (0.980)
  Pallas kernels: 43.8 us -> 42.9 us
    pallas_call x1, Pallas kernels: 43.8 us -> 42.9 us  [on_device(): pl.pallas_call(kernel, out_shape=jax.ShapeDtypeStruct((4, 128), jnp.float...]
where the time goes in v6:
time: 43.6 us; the launch traced here: 43.5 us
  Pallas kernels  42.9 us (98%)
  local copies, waits for them, and re-layouts  0.58 us (1%)
    pallas_call x1, Pallas kernels, on_device(): pl.pallas_call(kernel, out_shape=jax.ShapeDtypeStruct((4, 128), jnp.float...  42.9 us

profile of v6, /device:TPU:1, one launch (start us, length us, event | category | flops | bytes accessed | tf_op | source)
XLA Modules:
  0.0 43.5 jit_solution(1553100082768696608)
XLA Ops:
  0.0 42.9 %best_match.1 = f32[4,128]{1,0:T(4,128)S(1)} custom-call(f32[4,128,768]{2,1,0:T(8,128)} %bitcast.4, s32[128,128]{1,0:T(8,128)} %bitcast.5), custom_call_target="tpu_custom_call" | custom-call | flops 7000000000 | bytes 2000000 | tf_op jit(solution)/shard_map/best_match/pallas_call | solution.py:420
  42.9 0.6 %copy.4 = f32[1,512]{1,0:T(1,128)} copy(f32[1,512]{1,0:T(1,128)S(1)} %bitcast.3) | data formatting | bytes 4096

commit v7 on v6

--- a/solution.py
+++ b/solution.py
@@ -28,26 +28,26 @@
 HOLD = [[0, 3, 4, 5, 15], [1, 2, 4, 5, 14], [2, 1, 3, 6, 13], [3, 0, 2, 7, 12], [4, 3, 7, 8, 9], [5, 2, 6, 8, 9],
         [6, 1, 5, 7, 11], [7, 0, 4, 6, 10], [8, 4, 11, 12, 13], [9, 5, 10, 12, 13], [10, 2, 8, 11, 14],
         [11, 3, 9, 10, 15], [12, 0, 1, 8, 15], [13, 0, 1, 9, 14], [14, 6, 10, 13, 15], [15, 7, 11, 12, 14]]
-PAIRS = [[[(2, 4), (3, 4), (3, 1)], [(0, 2), (0, 3), (2, 3)]], [[(3, 2), (3, 4), (2, 4)], [(0, 1), (1, 3), (0, 3)]],
-         [[(2, 1), (1, 3), (2, 3)], [(0, 4), (1, 4), (3, 4)]], [[(1, 2), (2, 3), (3, 4)], [(2, 0), (2, 4), (0, 4)]],
+PAIRS = [[[(2, 4), (3, 4), (4, 1)], [(0, 2), (3, 1), (0, 3)]], [[(3, 2), (3, 4)], [(0, 1), (1, 3), (0, 3)]],
+         [[(2, 1), (1, 3), (3, 4)], [(0, 1), (0, 4), (1, 4)]], [[(1, 2), (2, 3), (2, 4)], [(0, 4), (3, 4)]],
          [[(2, 3), (1, 2), (1, 3)], [(4, 3), (4, 0), (1, 0), (4, 1)]],
-         [[(1, 3), (2, 1), (2, 3)], [(4, 3), (0, 3), (2, 0)]],
-         [[(4, 1), (4, 2), (2, 3)], [(2, 1), (0, 1), (2, 0), (0, 3)]],
-         [[(4, 2), (1, 2), (2, 3)], [(4, 1), (1, 0), (0, 3)]],
+         [[(1, 3), (2, 1), (2, 3)], [(4, 3), (4, 0), (0, 3), (2, 0)]],
+         [[(4, 1), (4, 2), (2, 3)], [(2, 1), (2, 0), (0, 1), (0, 3)]],
+         [[(4, 2), (1, 2), (2, 3)], [(4, 1), (4, 0), (1, 0), (0, 3)]],
          [[(4, 3), (4, 2), (2, 3)], [(4, 0), (1, 0), (1, 3), (4, 1)]],
          [[(4, 3), (4, 1), (1, 3)], [(0, 3), (2, 0), (2, 3)]], [[(2, 1), (4, 2), (4, 1)], [(2, 0), (4, 0), (4, 3)]],
-         [[(1, 0), (4, 1), (4, 0)], [(1, 2), (2, 0), (4, 2)]], [[(4, 2), (3, 4), (3, 1)], [(4, 0), (1, 0), (1, 2)]],
+         [[(1, 0), (4, 1), (4, 0)], [(1, 2), (2, 0), (4, 2)]], [[(4, 0), (3, 4), (3, 1)], [(4, 2), (1, 0), (1, 2)]],
          [[(3, 2), (3, 4), (2, 4)], [(4, 1), (2, 0), (2, 1)]], [[(4, 2), (2, 1), (4, 1)], [(4, 0), (2, 0), (3, 4)]],
-         [[(4, 1), (1, 2), (4, 2)], [(1, 0), (2, 0), (4, 0)]]]
-EARLY = [[1, 1], [0, 1], [1, 0], [1, 1], [1, 2], [1, 2], [2, 3], [2, 2], [1, 1], [1, 1], [1, 1], [1, 2], [1, 1],
+         [[(4, 1), (1, 2), (4, 2)], [(1, 0), (4, 0), (2, 0)]]]
+EARLY = [[1, 1], [0, 1], [1, 1], [1, 0], [1, 2], [1, 3], [2, 3], [2, 3], [1, 1], [1, 1], [1, 1], [1, 2], [1, 1],
          [0, 1], [3, 2], [3, 3]]
-NEED = [[[1, 2, 3, 4], [0, 2, 3]], [[2, 3, 4], [0, 1, 3]], [[1, 2, 3], [0, 1, 3, 4]], [[1, 2, 3, 4], [0, 2, 4]],
+NEED = [[[1, 2, 3, 4], [0, 1, 2, 3]], [[2, 3, 4], [0, 1, 3]], [[1, 2, 3, 4], [0, 1, 4]], [[1, 2, 3, 4], [0, 3, 4]],
         [[1, 2, 3], [0, 1, 3, 4]], [[1, 2, 3], [0, 2, 3, 4]], [[1, 2, 3, 4], [0, 1, 2, 3]],
         [[1, 2, 3, 4], [0, 1, 3, 4]], [[2, 3, 4], [0, 1, 3, 4]], [[1, 3, 4], [0, 2, 3]], [[1, 2, 4], [0, 2, 3, 4]],
-        [[0, 1, 4], [0, 1, 2, 4]], [[1, 2, 3, 4], [0, 1, 2, 4]], [[2, 3, 4], [0, 1, 2, 4]],
+        [[0, 1, 4], [0, 1, 2, 4]], [[0, 1, 3, 4], [0, 1, 2, 4]], [[2, 3, 4], [0, 1, 2, 4]],
         [[1, 2, 4], [0, 2, 3, 4]], [[1, 2, 4], [0, 1, 2, 4]]]
 
-REL = (0, 3, 1, 2)
+REL = (0, 1, 3, 2)
 
 
 def word(digits, base):
@@ -121,7 +121,7 @@
     ids_from = device(2 * h + 1 - zl, zh, p)
 
     def load(k):
-        return pltpu.make_async_copy(emb.at[group_of((z + pick((0, 1, 3, 2), k)) % 4)], stage.at[k], load_sem.at[k])
+        return pltpu.make_async_copy(emb.at[group_of((z + pick((0, 3, 1, 2), k)) % 4)], stage.at[k], load_sem.at[k])
 
     for k in range(4):
         load(k).start()
@@ -166,7 +166,7 @@
     def swap(k, half):
         rows = pl.ds(pl.multiple_of(k * 256 + h * 128 + half * 64, 64), 64)
         return remote(units.at[k - 1, pl.ds(half * 64, 64), :], x.at[0, rows, :], z_send.at[k - 1, half],
-                      z_recv.at[k - 1, half], device((z + pick((1, 3), k - 1)) % 4, h, p))
+                      z_recv.at[k - 1, half], device((z + pick((3, 1), k - 1)) % 4, h, p))
 
     between = device((z + jnp.where(h == 0, 1, 3)) % 4, h, p)
 

time: 43.6 us -> 45 us (1.032)
  Pallas kernels: 42.9 us -> 44.2 us
    pallas_call x1, Pallas kernels: 42.9 us -> 44.2 us  [on_device(): pl.pallas_call(kernel, out_shape=jax.ShapeDtypeStruct((4, 128), jnp.float...]
where the time goes in v7:
time: 45 us; the launch traced here: 44.8 us
  Pallas kernels  44.2 us (98%)
  local copies, waits for them, and re-layouts  0.58 us (1%)
    pallas_call x1, Pallas kernels, on_device(): pl.pallas_call(kernel, out_shape=jax.ShapeDtypeStruct((4, 128), jnp.float...  44.2 us

profile of v7, /device:TPU:1, one launch (start us, length us, event | category | flops | bytes accessed | tf_op | source)
XLA Modules:
  0.0 44.8 jit_solution(415015755832892910)
XLA Ops:
  0.0 44.2 %best_match.1 = f32[4,128]{1,0:T(4,128)S(1)} custom-call(f32[4,128,768]{2,1,0:T(8,128)} %bitcast.4, s32[128,128]{1,0:T(8,128)} %bitcast.5), custom_call_target="tpu_custom_call" | custom-call | flops 7000000000 | bytes 2000000 | tf_op jit(solution)/shard_map/best_match/pallas_call | solution.py:420
  44.3 0.6 %copy.4 = f32[1,512]{1,0:T(1,128)} copy(f32[1,512]{1,0:T(1,128)S(1)} %bitcast.3) | data formatting | bytes 4096

commit v8 on v7

--- a/solution.py
+++ b/solution.py
@@ -49,6 +49,9 @@
 
 REL = (0, 1, 3, 2)
 
+GROUP_OF = (2, 0, 1, 3)
+PLANE_OF = (1, 2, 0, 3)
+
 
 def word(digits, base):
     total = 0
@@ -92,7 +95,7 @@
         return ((z_of % 2) * 2 + core, chip * 2 + z_of // 2)
 
     def group_of(z_of):
-        return (1 - z_of % 2) * 2 + z_of // 2
+        return pick(GROUP_OF, z_of)
 
     near = [py * 4 + (px + 1) % 4, py * 4 + (px + 3) % 4, ((py + 1) % 4) * 4 + px, ((py + 3) % 4) * 4 + px]
     first = look_up(p, [word(SRC[c], 8) + 4096 * word(DEP[c], 4) for c in range(16)])
@@ -117,9 +120,9 @@
 
     sibling = device(z, 1 - h, p)
     owner_grp = group_of(z)
-    from_z = 2 * h + 1 - zl
-    ids_from = device(2 * h + 1 - zl, zh, p)
-
+    from_z = pick(PLANE_OF, grp)
+    ids_from = device(owner_grp // 2 + 2 * h, owner_grp % 2, p)
+    mine = grp == owner_grp
     def load(k):
         return pltpu.make_async_copy(emb.at[group_of((z + pick((0, 3, 1, 2), k)) % 4)], stage.at[k], load_sem.at[k])
 
@@ -131,10 +134,18 @@
     for d in range(4):
         pl.semaphore_signal(barrier, inc=1, device_id=device(z, h, near[d]), device_id_type=MESH)
     pl.semaphore_signal(barrier, inc=1, device_id=sibling, device_id_type=MESH)
-    pl.semaphore_signal(barrier, inc=1, device_id=ids_from, device_id_type=MESH)
     for k in range(SLOTS):
         for core in range(2):
-            pl.semaphore_signal(barrier, inc=1, device_id=device(from_z, core, holders[k]), device_id_type=MESH)
+            def tell():
+                pl.semaphore_signal(barrier, inc=1, device_id=device(from_z, core, holders[k]), device_id_type=MESH)
+            if k == 0:
+                pl.when(jnp.logical_not(jnp.logical_and(mine, h == core)))(tell)
+            else:
+                tell()
+
+    @pl.when(jnp.logical_not(mine))
+    def _():
+        pl.semaphore_signal(barrier, inc=1, device_id=ids_from, device_id_type=MESH)
 
     def normalised(k):
         v = stage[k]
@@ -144,7 +155,7 @@
     load(0).wait()
     own_rows = pl.multiple_of(h * 128, 128)
     x[0, pl.ds(own_rows, 128), :] = normalised(0)
-    pl.semaphore_wait(barrier, 18)
+    pl.semaphore_wait(barrier, jnp.where(mine, 16, 18))
 
     def remote(src_ref, dst_ref, send_sem, recv_sem, to):
         return pltpu.make_async_remote_copy(
@@ -220,7 +231,9 @@
             pl.when(k == 3)(lambda half=half: relay_in(half).start())
 
     ids_copy = remote(ids_in, ids_got, id_send, id_recv, device(from_z, zh, p))
-    ids_copy.start()
+    ids_here = pltpu.make_async_copy(ids_in, ids_got, id_recv)
+    pl.when(mine)(ids_here.start)
+    pl.when(jnp.logical_not(mine))(ids_copy.start)
     give(0, 0)
     give(0, 1)
     def strip(a, t, b, count, diagonal=False):
@@ -300,7 +313,8 @@
     swap(2, 0).wait_recv()
     own_piece_ready(4)
 
-    ids_copy.wait_recv()
+    pl.when(mine)(ids_here.wait)
+    pl.when(jnp.logical_not(mine))(ids_copy.wait_recv)
     ids_cols[...] = jnp.zeros_like(ids_cols)
     for s in range(SLOTS):
         for t in range(4):
@@ -385,9 +399,17 @@
         for half in range(2):
             copy = remote(part.at[s * 2 + half], parts_got.at[place[s] * 2 + h], r_send.at[s * 2 + half],
                           r_recv.at[place[s] * 2 + h], (owner_grp, held[s] * 2 + half))
-            copy.start()
-
-    ids_copy.wait_send()
+            if s == 0:
+                keep_it = jnp.logical_and(mine, zh == half)
+                pl.when(jnp.logical_not(keep_it))(copy.start)
+
+                @pl.when(keep_it)
+                def _():
+                    parts_got[h] = part[half]
+            else:
+                copy.start()
+
+    pl.when(jnp.logical_not(mine))(ids_copy.wait_send)
     for half in range(2):
         for copy in (swap(1, half), swap(2, half), relay_in(half), relay_out(half)):
             copy.wait_send()
@@ -402,7 +424,10 @@
     best = None
     for k in range(2 * SLOTS):
         got = remote(parts_got.at[k], parts_got.at[k], r_send.at[k], r_recv.at[k], sibling)
-        got.wait_recv()
+        if k < 2:
+            pl.when(jnp.logical_not(jnp.logical_and(mine, h == k)))(got.wait_recv)
+        else:
+            got.wait_recv()
         best = parts_got[k] if best is None else jnp.maximum(best, parts_got[k])
     out[...] = best
 
@@ -410,7 +435,10 @@
         for half in range(2):
             copy = remote(part.at[s * 2 + half], parts_got.at[place[s] * 2 + h], r_send.at[s * 2 + half],
                           r_recv.at[place[s] * 2 + h], (owner_grp, held[s] * 2 + half))
-            copy.wait_send()
+            if s == 0:
+                pl.when(jnp.logical_not(jnp.logical_and(mine, zh == half)))(copy.wait_send)
+            else:
+                copy.wait_send()
 
 
 def on_device(embeddings, cluster_ids):

time: 45 us -> 45.3 us (level)
  no operation moved by 1% of the time
where the time goes in v8:
time: 45.3 us; the launch traced here: 45.1 us
  Pallas kernels  44.6 us (98%)
  local copies, waits for them, and re-layouts  0.58 us (1%)
    pallas_call x1, Pallas kernels, on_device(): pl.pallas_call(kernel, out_shape=jax.ShapeDtypeStruct((4, 128), jnp.float...  44.6 us

profile of v8, /device:TPU:1, one launch (start us, length us, event | category | flops | bytes accessed | tf_op | source)
XLA Modules:
  0.0 45.1 jit_solution(2384497405967314982)
XLA Ops:
  0.0 44.6 %best_match.1 = f32[4,128]{1,0:T(4,128)S(1)} custom-call(f32[4,128,768]{2,1,0:T(8,128)} %bitcast.4, s32[128,128]{1,0:T(8,128)} %bitcast.5), custom_call_target="tpu_custom_call" | custom-call | flops 7000000000 | bytes 2000000 | tf_op jit(solution)/shard_map/best_match/pallas_call | solution.py:448
  44.6 0.6 %copy.4 = f32[1,512]{1,0:T(1,128)} copy(f32[1,512]{1,0:T(1,128)S(1)} %bitcast.3) | data formatting | bytes 4096

commit v9 on v6

--- a/solution.py
+++ b/solution.py
@@ -47,7 +47,8 @@
         [[0, 1, 4], [0, 1, 2, 4]], [[1, 2, 3, 4], [0, 1, 2, 4]], [[2, 3, 4], [0, 1, 2, 4]],
         [[1, 2, 4], [0, 2, 3, 4]], [[1, 2, 4], [0, 1, 2, 4]]]
 
-REL = (0, 3, 1, 2)
+REL = (0, 1, 3, 2)
+LAST = 3
 
 
 def word(digits, base):
@@ -120,14 +121,16 @@
     from_z = 2 * h + 1 - zl
     ids_from = device(2 * h + 1 - zl, zh, p)
 
+    rel = [jnp.where(z == LAST, REL[t] if t in (0, 3) else REL[3 - t], REL[t]) for t in range(4)]
+
     def load(k):
-        return pltpu.make_async_copy(emb.at[group_of((z + pick((0, 1, 3, 2), k)) % 4)], stage.at[k], load_sem.at[k])
+        return pltpu.make_async_copy(emb.at[group_of((z + pick((0, 3, 1, 2), k)) % 4)], stage.at[k], load_sem.at[k])
 
     for k in range(4):
         load(k).start()
     barrier = pltpu.get_barrier_semaphore()
-    for rel in (1, 3):
-        pl.semaphore_signal(barrier, inc=1, device_id=device((z + rel) % 4, h, p), device_id_type=MESH)
+    for step in (1, 3):
+        pl.semaphore_signal(barrier, inc=1, device_id=device((z + step) % 4, h, p), device_id_type=MESH)
     for d in range(4):
         pl.semaphore_signal(barrier, inc=1, device_id=device(z, h, near[d]), device_id_type=MESH)
     pl.semaphore_signal(barrier, inc=1, device_id=sibling, device_id_type=MESH)
@@ -164,9 +167,16 @@
                       device(z, h, near[s - 1]))
 
     def swap(k, half):
-        rows = pl.ds(pl.multiple_of(k * 256 + h * 128 + half * 64, 64), 64)
+        z_to = (z + pick((3, 1), k - 1)) % 4
+        t = jnp.where(z_to == LAST, 3 - k, k)
+        rows = pl.ds(pl.multiple_of(t * 256 + h * 128 + half * 64, 64), 64)
         return remote(units.at[k - 1, pl.ds(half * 64, 64), :], x.at[0, rows, :], z_send.at[k - 1, half],
-                      z_recv.at[k - 1, half], device((z + pick((1, 3), k - 1)) % 4, h, p))
+                      z_recv.at[t - 1, half], device(z_to, h, p))
+
+    def swapped(t, half):
+        rows = pl.ds(pl.multiple_of(t * 256 + h * 128 + half * 64, 64), 64)
+        return remote(units.at[t - 1, pl.ds(half * 64, 64), :], x.at[0, rows, :], z_send.at[t - 1, half],
+                      z_recv.at[t - 1, half], device((z + 1) % 4, h, p))
 
     between = device((z + jnp.where(h == 0, 1, 3)) % 4, h, p)
 
@@ -292,12 +302,12 @@
         give_held(2, t)
 
     pass_on(1)
-    swap(1, 0).wait_recv()
+    swapped(1, 0).wait_recv()
     own_piece_ready(2)
     pass_on(2)
-    swap(1, 1).wait_recv()
+    swapped(1, 1).wait_recv()
     own_piece_ready(3)
-    swap(2, 0).wait_recv()
+    swapped(2, 0).wait_recv()
     own_piece_ready(4)
 
     ids_copy.wait_recv()
@@ -305,7 +315,7 @@
     for s in range(SLOTS):
         for t in range(4):
             for core in range(2):
-                unit = held[s] * 8 + 2 * ((z + REL[t]) % 4) + core
+                unit = held[s] * 8 + 2 * ((z + rel[t]) % 4) + core
                 ids_cols[pl.ds(s * 8 + 2 * t + core, 1), :] = ids_got[pl.ds(unit, 1), :].astype(jnp.float32)
     turned = ids_cols[...].T
     for j in range(SLOTS * 8):
@@ -315,7 +325,7 @@
     for half in range(2):
         relay_in(half).wait_recv()
         relay_out(half).start()
-    swap(2, 1).wait_recv()
+    swapped(2, 1).wait_recv()
     own_piece_ready(5)
     @pl.loop(0, SLOTS * 8)
     def _(j):
@@ -377,7 +387,7 @@
 
     for s in range(SLOTS):
         for t in range(4):
-            z_of = (z + REL[t]) % 4
+            z_of = (z + rel[t]) % 4
             for core in range(2):
                 j = s * 8 + 2 * t + core
                 both = jnp.maximum(row_line[j:j + 1, :], jnp.max(col_best[j], axis=0, keepdims=True))

time: 43.6 us -> 44 us (level)
  no operation moved by 1% of the time
where the time goes in v9:
time: 44 us; the launch traced here: 43.8 us
  Pallas kernels  43.2 us (98%)
  local copies, waits for them, and re-layouts  0.58 us (1%)
    pallas_call x1, Pallas kernels, on_device(): pl.pallas_call(kernel, out_shape=jax.ShapeDtypeStruct((4, 128), jnp.float...  43.2 us

profile of v9, /device:TPU:1, one launch (start us, length us, event | category | flops | bytes accessed | tf_op | source)
XLA Modules:
  0.0 43.8 jit_solution(11164202426953113615)
XLA Ops:
  0.0 43.2 %best_match.1 = f32[4,128]{1,0:T(4,128)S(1)} custom-call(f32[4,128,768]{2,1,0:T(8,128)} %bitcast.4, s32[128,128]{1,0:T(8,128)} %bitcast.5), custom_call_target="tpu_custom_call" | custom-call | flops 7000000000 | bytes 2000000 | tf_op jit(solution)/shard_map/best_match/pallas_call | solution.py:430
  43.3 0.6 %copy.4 = f32[1,512]{1,0:T(1,128)} copy(f32[1,512]{1,0:T(1,128)S(1)} %bitcast.3) | data formatting | bytes 4096

commit v10 on v9

--- a/solution.py
+++ b/solution.py
@@ -383,9 +383,12 @@
             take(6)
             finish_rows(2)
             take(7)
-    finish_rows(3)
-
     for s in range(SLOTS):
+        for core in range(2):
+            unit = s * 8 + 6 + core
+            row_line[unit:unit + 1, :] = jnp.max(row_best[unit].T, axis=0, keepdims=True)
+
+    for s in (1, 2, 3, 4, 0):
         for t in range(4):
             z_of = (z + rel[t]) % 4
             for core in range(2):

time: 44 us -> 43.8 us (level)
  no operation moved by 1% of the time
where the time goes in v10:
time: 43.8 us; the launch traced here: 43.7 us
  Pallas kernels  43.1 us (98%)
  local copies, waits for them, and re-layouts  0.58 us (1%)
    pallas_call x1, Pallas kernels, on_device(): pl.pallas_call(kernel, out_shape=jax.ShapeDtypeStruct((4, 128), jnp.float...  43.1 us

profile of v10, /device:TPU:1, one launch (start us, length us, event | category | flops | bytes accessed | tf_op | source)
XLA Modules:
  0.0 43.7 jit_solution(7439486540087365480)
XLA Ops:
  0.0 43.1 %best_match.1 = f32[4,128]{1,0:T(4,128)S(1)} custom-call(f32[4,128,768]{2,1,0:T(8,128)} %bitcast.4, s32[128,128]{1,0:T(8,128)} %bitcast.5), custom_call_target="tpu_custom_call" | custom-call | flops 7000000000 | bytes 2000000 | tf_op jit(solution)/shard_map/best_match/pallas_call | solution.py:433
  43.1 0.6 %copy.4 = f32[1,512]{1,0:T(1,128)} copy(f32[1,512]{1,0:T(1,128)S(1)} %bitcast.3) | data formatting | bytes 4096

commit v11 on v6

--- a/solution.py
+++ b/solution.py
@@ -373,9 +373,12 @@
             take(6)
             finish_rows(2)
             take(7)
-    finish_rows(3)
-
     for s in range(SLOTS):
+        for core in range(2):
+            unit = s * 8 + 6 + core
+            row_line[unit:unit + 1, :] = jnp.max(row_best[unit].T, axis=0, keepdims=True)
+
+    for s in (1, 2, 3, 4, 0):
         for t in range(4):
             z_of = (z + REL[t]) % 4
             for core in range(2):

time: 43.6 us -> 43.5 us (level)
  no operation moved by 1% of the time
where the time goes in v11:
time: 43.5 us; the launch traced here: 43.4 us
  Pallas kernels  42.8 us (98%)
  local copies, waits for them, and re-layouts  0.58 us (1%)
    pallas_call x1, Pallas kernels, on_device(): pl.pallas_call(kernel, out_shape=jax.ShapeDtypeStruct((4, 128), jnp.float...  42.8 us

profile of v11, /device:TPU:1, one launch (start us, length us, event | category | flops | bytes accessed | tf_op | source)
XLA Modules:
  0.0 43.4 jit_solution(1239091411453045160)
XLA Ops:
  0.0 42.8 %best_match.1 = f32[4,128]{1,0:T(4,128)S(1)} custom-call(f32[4,128,768]{2,1,0:T(8,128)} %bitcast.4, s32[128,128]{1,0:T(8,128)} %bitcast.5), custom_call_target="tpu_custom_call" | custom-call | flops 7000000000 | bytes 2000000 | tf_op jit(solution)/shard_map/best_match/pallas_call | solution.py:423
  42.8 0.6 %copy.4 = f32[1,512]{1,0:T(1,128)} copy(f32[1,512]{1,0:T(1,128)S(1)} %bitcast.3) | data formatting | bytes 4096

commit v12 on v7

--- a/solution.py
+++ b/solution.py
@@ -47,7 +47,7 @@
         [[0, 1, 4], [0, 1, 2, 4]], [[0, 1, 3, 4], [0, 1, 2, 4]], [[2, 3, 4], [0, 1, 2, 4]],
         [[1, 2, 4], [0, 2, 3, 4]], [[1, 2, 4], [0, 1, 2, 4]]]
 
-REL = (0, 1, 3, 2)
+REL = (0, 3, 1, 2)
 
 
 def word(digits, base):
@@ -121,7 +121,7 @@
     ids_from = device(2 * h + 1 - zl, zh, p)
 
     def load(k):
-        return pltpu.make_async_copy(emb.at[group_of((z + pick((0, 3, 1, 2), k)) % 4)], stage.at[k], load_sem.at[k])
+        return pltpu.make_async_copy(emb.at[group_of((z + pick((0, 1, 3, 2), k)) % 4)], stage.at[k], load_sem.at[k])
 
     for k in range(4):
         load(k).start()
@@ -166,7 +166,7 @@
     def swap(k, half):
         rows = pl.ds(pl.multiple_of(k * 256 + h * 128 + half * 64, 64), 64)
         return remote(units.at[k - 1, pl.ds(half * 64, 64), :], x.at[0, rows, :], z_send.at[k - 1, half],
-                      z_recv.at[k - 1, half], device((z + pick((3, 1), k - 1)) % 4, h, p))
+                      z_recv.at[k - 1, half], device((z + pick((1, 3), k - 1)) % 4, h, p))
 
     between = device((z + jnp.where(h == 0, 1, 3)) % 4, h, p)
 
@@ -373,9 +373,12 @@
             take(6)
             finish_rows(2)
             take(7)
-    finish_rows(3)
-
     for s in range(SLOTS):
+        for core in range(2):
+            unit = s * 8 + 6 + core
+            row_line[unit:unit + 1, :] = jnp.max(row_best[unit].T, axis=0, keepdims=True)
+
+    for s in (1, 2, 3, 4, 0):
         for t in range(4):
             z_of = (z + REL[t]) % 4
             for core in range(2):

time: 45 us -> 43.5 us (0.967)
  Pallas kernels: 44.2 us -> 42.8 us
    pallas_call x1, Pallas kernels: 44.2 us -> 42.8 us  [on_device(): pl.pallas_call(kernel, out_shape=jax.ShapeDtypeStruct((4, 128), jnp.float...]
where the time goes in v12:
time: 43.5 us; the launch traced here: 43.4 us
  Pallas kernels  42.8 us (98%)
  local copies, waits for them, and re-layouts  0.58 us (1%)
    pallas_call x1, Pallas kernels, on_device(): pl.pallas_call(kernel, out_shape=jax.ShapeDtypeStruct((4, 128), jnp.float...  42.8 us

profile of v12, /device:TPU:1, one launch (start us, length us, event | category | flops | bytes accessed | tf_op | source)
XLA Modules:
  0.0 43.4 jit_solution(11957303443662491139)
XLA Ops:
  0.0 42.8 %best_match.1 = f32[4,128]{1,0:T(4,128)S(1)} custom-call(f32[4,128,768]{2,1,0:T(8,128)} %bitcast.4, s32[128,128]{1,0:T(8,128)} %bitcast.5), custom_call_target="tpu_custom_call" | custom-call | flops 7000000000 | bytes 2000000 | tf_op jit(solution)/shard_map/best_match/pallas_call | solution.py:423
  42.8 0.6 %copy.4 = f32[1,512]{1,0:T(1,128)} copy(f32[1,512]{1,0:T(1,128)S(1)} %bitcast.3) | data formatting | bytes 4096
